TPU v7x, 32 devices: a whole 2x2x4 slice. The times are simulated.
32 devices in a mesh: groups: 2 (over x), ctx: 16 (over z, y, core).
Axes of the slice: x: 2, y: 2, z: 4, core: 2. Of those that a mesh axis runs over, the one named last changes fastest.
Arguments:
- queries: bfloat16 [4096, 4096], P(('groups', 'ctx')), parts along dimension 0, may hold values from -6 to 6
- key_input: bfloat16 [4096, 4096], P(('groups', 'ctx')), parts along dimension 0, may hold values from -6 to 6
- value_input: bfloat16 [4096, 4096], P(('groups', 'ctx')), parts along dimension 0, may hold values from -6 to 6
- log_decay: float32 [4096, 32], P(('groups', 'ctx')), parts along dimension 0, may hold values from -2.5 to 0
- conv_weight: float32 [4, 4096], replicated, may hold values from -3 to 3
- norm_gain: float32 [4096], replicated, may hold values from 0.1 to 1.9
Outputs:
- mixed_out: bfloat16 [4096, 4096], P(('groups', 'ctx')), parts along dimension 0
There are 2 independent parts, one for each index of `groups`. A program takes and returns all parts, laid end to end along the dimension named above; an argument that names none is the same for every part. Nothing has to cross between parts.
All inputs are finite; a program needn't handle non-finite values.
Results may differ from a plain program's by a relative error of at most 0.0066.
Values may be sent and summed in bfloat16 or wider, within the bound.
A program may use at most 320 MiB of HBM per device.

v0:
```python
import jax
import jax.numpy as jnp
from jax import lax
from jax.sharding import PartitionSpec as P


def from_behind(block, axis, distance):
    devices = range(lax.axis_size(axis))
    route = [(i - distance, i) for i in devices if i - distance in devices]
    return lax.ppermute(block, axis, route)


def join_rows(earlier, later):
    return (earlier[0] * later[0], later[0][..., None] * earlier[1] + later[1])


def block_prefix(states, rates):
    carried = lax.associative_scan(join_rows, (rates, states), axis=0)
    inclusive = carried[1]
    return jnp.concatenate([jnp.zeros_like(inclusive[:1]), inclusive[:-1]], 0)


def on_device(queries, key_input, value_input, log_decay, conv_weight, norm_gain):
    row_count, width_all = queries.shape
    head_count = log_decay.shape[1]
    head_size = width_all // head_count
    taps = conv_weight.shape[0]
    key_tail = from_behind(key_input[row_count - (taps - 1) :], "ctx", 1)
    extended = jnp.concatenate([key_tail, key_input], 0)
    conv_sum = jnp.zeros((row_count, width_all), jnp.float32)
    for offset in range(taps):
        start = taps - 1 - offset
        conv_sum = conv_sum + conv_weight[offset][None, :] * extended[
            start : start + row_count
        ].astype(jnp.float32)
    key_conv = conv_sum.astype(jnp.bfloat16).reshape(row_count, head_count, head_size)
    query_heads = queries.reshape(row_count, head_count, head_size)
    value_heads = value_input.reshape(row_count, head_count, head_size)
    cum = jnp.cumsum(log_decay, axis=0)
    total = cum[-1]
    cum_heads = cum.T
    causal = jnp.arange(row_count)[:, None] >= jnp.arange(row_count)[None, :]
    scores = jnp.einsum("thd,shd->hts", query_heads, key_conv, preferred_element_type=jnp.float32)
    spread = cum_heads[:, :, None] - cum_heads[:, None, :]
    weights = jnp.where(
        causal[None], scores * jnp.exp(jnp.where(causal[None], spread, 0.0)), 0.0
    ).astype(jnp.bfloat16)
    intra = jnp.einsum("hts,shd->thd", weights, value_heads, preferred_element_type=jnp.float32)
    weighted_keys = (
        key_conv.astype(jnp.float32) * jnp.exp(total[None, :] - cum)[:, :, None]
    ).astype(jnp.bfloat16)
    block_state = jnp.einsum(
        "shd,she->hde", weighted_keys, value_heads, preferred_element_type=jnp.float32
    )
    decay_block = jnp.exp(total)
    stacked = block_state.reshape(1, head_count * head_size, head_size)
    row_decay = jnp.repeat(decay_block, head_size).reshape(1, head_count * head_size)
    received = (
        lax.all_to_all(stacked, "ctx", split_axis=1, concat_axis=0, tiled=True),
        lax.all_to_all(row_decay, "ctx", split_axis=1, concat_axis=0, tiled=True),
    )
    shared = block_prefix(received[0], received[1])
    returned = lax.all_to_all(
        shared.astype(jnp.bfloat16), "ctx", split_axis=0, concat_axis=1, tiled=True
    ).astype(shared.dtype)
    prefix = returned.reshape(head_count, head_size, head_size)
    prefix_low = prefix.astype(jnp.bfloat16)
    inter = (
        jnp.einsum("thd,hde->the", query_heads, prefix_low, preferred_element_type=jnp.float32)
        * jnp.exp(cum)[:, :, None]
    )
    mixed = intra + inter
    scale_inv = lax.rsqrt(jnp.mean(mixed * mixed, axis=2, keepdims=True) + 1e-05)
    gain_heads = norm_gain.reshape(head_count, head_size)
    result = (mixed * scale_inv * gain_heads[None]).astype(jnp.bfloat16)
    return result.reshape(row_count, width_all)


def solution(mesh):
    return jax.shard_map(
        on_device,
        mesh=mesh,
        in_specs=(
            P(("groups", "ctx"), None),
            P(("groups", "ctx"), None),
            P(("groups", "ctx"), None),
            P(("groups", "ctx"), None),
            P(),
            P(),
        ),
        out_specs=P(("groups", "ctx"), None),
        check_vma=False,
    )
```

profile of v0, /device:TPU:27, one launch (start us, length us, event | category | flops | bytes accessed | tf_op | source)
XLA Modules:
  0.0 146.2 jit_solution(7844349312918292314)
XLA Ops:
  0.0 0.9 slice.123
  1.0 3.7 %collective-permute-start = (bf16[3,4096]{1,0:T(4,128)(2,1)S(1)}, bf16[3,4096]{1,0:T(4,128)(2,1)S(1)}, u32[]{:S(2)}, u32[]{:S(2)}) collective-permute-start(bf16[3,4096]{1,0:T(4,128)(2,1)S(1)} %slice.123), channel_id=1, source_target_pairs={{0,1},{1,2},{2,3},{3,4},{4,5},{5,6},{6,7},{7,8},{8,9},{9,10},{10,1... | collective-permute-start | bytes 73736 | tf_op jit(solution)/shard_map/ppermute | solution.py:10
  4.7 0.8 copy.30
  5.8 0.7 broadcast_in_dim.24
  6.5 4.9 %all-to-all-start.1 = ((f32[1,16,256]{2,0,1:T(1,128)}), f32[1,16,256]{2,0,1:T(1,128)S(1)}, u32[]{:S(2)}, u32[]{:S(2)}) async-start(f32[1,16,256]{2,0,1:T(1,128)} %bitcast.12), calls=%async_computation.1 | async-start | bytes 32768 | tf_op jit(solution)/shard_map/all_to_all | solution.py:60
  11.3 1.1 fusion.31
  12.4 0.6 fusion.30
  13.1 4.0 %add_convert_fusion = bf16[128,4096]{1,0:T(8,128)(2,1)S(1)} fusion(bf16[128,4096]{1,0:T(8,128)(2,1)} %param.7, bf16[3,4096]{1,0:T(4,128)(2,1)S(1)} %collective-permute-done, f32[4096]{0:T(1024)S(1)} %bitcast.86, f32[4096]{0:T(1024)S(1)} %bitcast.87, f32[4096]{0:T(1024)S(1)} %bitcast.85, f32[4096]{0:T(1024)S(1)} %bitcast.84), kind=kLoop, calls=%fused_computation.8 | loop fusion | flops 11010048 | bytes 2187264 | tf_op jit(solution)/shard_map/convert_element_type | solution.py:36
  17.1 0.7 copy.46
  17.8 1.8 %fusion.5 = f32[32,128,128]{2,1,0:T(8,128)} fusion(bf16[128,32,128]{0,2,1:T(8,128)(2,1)S(1)} %bitcast.77, f32[128,32]{0,1:T(8,128)S(1)} %copy.36, bf16[128,4096]{1,0:T(8,128)(2,1)S(1)} %copy-done), kind=kOutput, calls=%fused_computation.14 | convolution fusion | flops 135790592 | bytes 4210688 | tf_op jit(solution)/shard_map/shd,she->hde/dot_general | solution.py:52
  19.6 6.0 %all-to-all-start = ((f32[1,4096,128]{2,0,1:T(1,128)}), f32[1,4096,128]{2,0,1:T(1,128)S(1)}, u32[]{:S(2)}, u32[]{:S(2)}) async-start(f32[1,4096,128]{2,0,1:T(1,128)} %bitcast.75), calls=%async_computation | async-start | bytes 4194304 | tf_op jit(solution)/shard_map/all_to_all | solution.py:59
  25.8 43.9 %all-to-all-done = f32[1,4096,128]{2,0,1:T(1,128)S(1)} async-done(((f32[1,4096,128]{2,0,1:T(1,128)}), f32[1,4096,128]{2,0,1:T(1,128)S(1)}, u32[]{:S(2)}, u32[]{:S(2)}) %all-to-all-start) | async-done | bytes 2097184 | tf_op jit(solution)/shard_map/all_to_all | solution.py:59
  70.3 0.8 slice_bitcast_fusion
  71.5 0.7 pad_maximum_fusion.3
  72.2 2.4 %pad.29 = f32[4,256,128]{2,1,0:T(8,128)} pad(f32[2,256,128]{2,1,0:T(8,128)} %pad_maximum_fusion.3, f32[]{:T(128)} %constant.4.clone.1), padding=0_1_1x0_0_0x0_0_0 | pad | bytes 786436 | tf_op jit(solution)/shard_map/pad | solution.py:18
  74.7 1.5 %pad.30 = f32[4,256,128]{2,1,0:T(8,128)} pad(f32[2,256,128]{2,1,0:T(8,128)S(1)} %pad_add_fusion, f32[]{:T(128)} %constant.4.clone.1), padding=1_0_1x0_0_0x0_0_0 | pad | bytes 786436 | tf_op jit(solution)/shard_map/pad | solution.py:18
  76.2 2.1 %add.83 = f32[4,256,128]{2,1,0:T(8,128)} add(f32[4,256,128]{2,1,0:T(8,128)} %pad.29, f32[4,256,128]{2,1,0:T(8,128)} %pad.30) | non-fusion elementwise | flops 131072 | bytes 1572864 | tf_op jit(solution)/shard_map/add | solution.py:18
  78.3 1.4 fusion.23
  79.7 0.8 pad_maximum_fusion.2
  80.5 4.1 %pad.31 = f32[8,256,128]{2,1,0:T(8,128)} pad(f32[4,256,128]{2,1,0:T(8,128)} %pad_maximum_fusion.2, f32[]{:T(128)} %constant.4.clone.1), padding=0_1_1x0_0_0x0_0_0 | pad | bytes 1572868 | tf_op jit(solution)/shard_map/pad | solution.py:18
  84.6 4.1 %pad.32 = f32[8,256,128]{2,1,0:T(8,128)} pad(f32[4,256,128]{2,1,0:T(8,128)} %add.83, f32[]{:T(128)} %constant.4.clone.1), padding=1_0_1x0_0_0x0_0_0 | pad | bytes 1572868 | tf_op jit(solution)/shard_map/pad | solution.py:18
  88.8 2.8 %add.85 = f32[8,256,128]{2,1,0:T(8,128)} add(f32[8,256,128]{2,1,0:T(8,128)} %pad.31, f32[8,256,128]{2,1,0:T(8,128)} %pad.32) | non-fusion elementwise | flops 262144 | bytes 3145728 | tf_op jit(solution)/shard_map/add | solution.py:18
  92.5 4.0 %pad.46 = f32[15,256,128]{2,1,0:T(8,128)} pad(f32[8,256,128]{2,1,0:T(8,128)S(1)} %pad_maximum_fusion.1, f32[]{:T(128)} %constant.4.clone.1), padding=0_0_1x0_0_0x0_0_0 | pad | bytes 3014660 | tf_op jit(solution)/shard_map/slice | solution.py:20
  96.6 3.9 %pad.81 = f32[16,256,128]{2,1,0:T(8,128)S(1)} pad(f32[8,256,128]{2,1,0:T(8,128)} %add.85, f32[]{:T(128)} %constant.4.clone.1), padding=1_0_1x0_0_0x0_0_0 | pad | bytes 3145732
  100.5 1.8 %add_convert_fusion.1 = bf16[15,256,128]{2,1,0:T(8,128)(2,1)S(1)} fusion(f32[15,256,128]{2,1,0:T(8,128)} %pad.46, f32[16,256,128]{2,1,0:T(8,128)S(1)} %pad.81), kind=kLoop, calls=%fused_computation.9 | loop fusion | flops 983040 | bytes 4915200 | tf_op jit(solution)/shard_map/convert.2
  102.2 1.1 concatenate.19
  103.3 8.2 %all-to-all-start.2 = ((bf16[16,256,128]{2,1,0:T(8,128)(2,1)}), bf16[16,256,128]{2,1,0:T(8,128)(2,1)S(1)}, u32[]{:S(2)}, u32[]{:S(2)}) async-start(bf16[16,256,128]{2,1,0:T(8,128)(2,1)} %concatenate.19), calls=%async_computation.2 | async-start | bytes 2097152 | tf_op jit(solution)/shard_map/all_to_all | solution.py:63
  111.7 22.8 %all-to-all-done.2 = bf16[16,256,128]{2,1,0:T(8,128)(2,1)S(1)} async-done(((bf16[16,256,128]{2,1,0:T(8,128)(2,1)}), bf16[16,256,128]{2,1,0:T(8,128)(2,1)S(1)}, u32[]{:S(2)}, u32[]{:S(2)}) %all-to-all-start.2) | async-done | bytes 1048608 | tf_op jit(solution)/shard_map/all_to_all | solution.py:63
  134.5 3.5 %fusion.6 = f32[32,128,128]{2,1,0:T(8,128)} fusion(bf16[32,128,128]{2,1,0:T(8,128)(2,1)S(1)} %bitcast.79, bf16[128,4096]{1,0:T(8,128)(2,1)} %param.6), kind=kOutput, calls=%fused_computation.15 | convolution fusion | flops 134217728 | bytes 4194304 | tf_op jit(solution)/shard_map/thd,hde->the/dot_general | solution.py:69
  138.1 4.9 %multiply_reduce_fusion = (f32[128,32]{0,1:T(8,128)S(1)}, f32[128,32,128]{0,2,1:T(8,128)}) fusion(f32[128,32]{0,1:T(8,128)S(1)} %copy.41, f32[32,128,128]{2,1,0:T(8,128)} %fusion.6, bf16[128,32,128]{0,2,1:T(8,128)(2,1)S(1)} %bitcast.78, f32[32,128]{1,0:T(8,128)S(1)} %copy.31, pred[128,128]{0,1:T(8,128)(4,1)S(1)} %iota_compare_fusion, ...), kind=kOutput, calls=%fused_computation.6 | convolution fusion | flops 273149952 | bytes 7405568 | tf_op jit(solution)/shard_map/hts,shd->thd/dot_general | solution.py:48
  143.0 1.9 %multiply_convert_fusion = bf16[128,32,128]{0,2,1:T(8,128)(2,1)S(1)} fusion(f32[128,32,128]{0,2,1:T(8,128)} %get-tuple-element.18, f32[32,128]{1,0:T(8,128)S(1)} %bitcast.88, f32[128,32]{0,1:T(8,128)S(1)} %add_rsqrt_fusion), kind=kLoop, calls=%fused_computation.5 | loop fusion | flops 1572864 | bytes 3178496 | tf_op jit(solution)/shard_map/convert_element_type | solution.py:75
  144.9 1.3 copy.42
  (55 shorter events, 2.6 us)
Async XLA Ops:
  0.0 17.8 %copy-start = (bf16[128,4096]{1,0:T(8,128)(2,1)S(1)}, bf16[128,4096]{1,0:T(8,128)(2,1)}, u32[]{:S(2)}) copy-start(bf16[128,4096]{1,0:T(8,128)(2,1)} %param.8) | copy-start | bytes 3145732
  1.0 12.2 %collective-permute-start = (bf16[3,4096]{1,0:T(4,128)(2,1)S(1)}, bf16[3,4096]{1,0:T(4,128)(2,1)S(1)}, u32[]{:S(2)}, u32[]{:S(2)}) collective-permute-start(bf16[3,4096]{1,0:T(4,128)(2,1)S(1)} %slice.123), channel_id=1, source_target_pairs={{0,1},{1,2},{2,3},{3,4},{4,5},{5,6},{6,7},{7,8},{8,9},{9,10},{10,1... | collective-permute-start | bytes 73736 | tf_op jit(solution)/shard_map/ppermute | solution.py:10
  5.7 7.5 %copy-start.6 = (f32[128,32]{1,0:T(8,128)}, f32[128,32]{1,0:T(8,128)S(1)}, u32[]{:S(2)}) copy-start(f32[128,32]{1,0:T(8,128)S(1)} %reduce_window_sum.11) | copy-start | bytes 49156
  6.5 13.1 %all-to-all-start.1 = ((f32[1,16,256]{2,0,1:T(1,128)}), f32[1,16,256]{2,0,1:T(1,128)S(1)}, u32[]{:S(2)}, u32[]{:S(2)}) async-start(f32[1,16,256]{2,0,1:T(1,128)} %bitcast.12), calls=%async_computation.1 | async-start | bytes 32768 | tf_op jit(solution)/shard_map/all_to_all | solution.py:60
  17.8 1.8 %copy-start.4 = (bf16[128,4096]{0,1:T(8,128)(2,1)}, bf16[128,4096]{0,1:T(8,128)(2,1)S(1)}, u32[]{:S(2)}) copy-start(bf16[128,4096]{0,1:T(8,128)(2,1)S(1)} %copy.46) | copy-start | bytes 3145732
  19.6 50.1 %all-to-all-start = ((f32[1,4096,128]{2,0,1:T(1,128)}), f32[1,4096,128]{2,0,1:T(1,128)S(1)}, u32[]{:S(2)}, u32[]{:S(2)}) async-start(f32[1,4096,128]{2,0,1:T(1,128)} %bitcast.75), calls=%async_computation | async-start | bytes 4194304 | tf_op jit(solution)/shard_map/all_to_all | solution.py:59
  70.1 1.4 copy-start.3
  74.6 5.0 %slice-start = ((f32[8,256,128]{2,1,0:T(8,128)}), f32[1,256,128]{2,1,0:T(8,128)S(1)}, s32[]{:S(2)}) async-start(f32[8,256,128]{2,1,0:T(8,128)} %copy-done.3), calls=%async_computation.3 | async-start | bytes 262144 | tf_op jit(solution)/shard_map/slice | solution.py:18
  88.7 2.8 %copy-start.1 = (f32[8,256,128]{2,1,0:T(8,128)S(1)}, f32[8,256,128]{2,1,0:T(8,128)}, u32[]{:S(2)}) copy-start(f32[8,256,128]{2,1,0:T(8,128)} %pad.31) | copy-start | bytes 3145732
  88.7 2.8 %copy-start.2 = (f32[8,256,128]{2,1,0:T(8,128)S(1)}, f32[8,256,128]{2,1,0:T(8,128)}, u32[]{:S(2)}) copy-start(f32[8,256,128]{2,1,0:T(8,128)} %pad.32) | copy-start | bytes 3145732
  91.6 0.9 copy-start.8
  102.2 9.3 %copy-start.7 = (f32[128,32]{1,0:T(8,128)S(1)}, f32[128,32]{1,0:T(8,128)}, u32[]{:S(2)}) copy-start(f32[128,32]{1,0:T(8,128)} %copy-done.6) | copy-start | bytes 49156
  102.2 9.4 %copy-start.9 = (f32[128,32]{1,0:T(8,128)S(1)}, f32[128,32]{1,0:T(8,128)}, u32[]{:S(2)}) copy-start(f32[128,32]{1,0:T(8,128)} %get-tuple-element.9) | copy-start | bytes 49156
  103.3 31.2 %all-to-all-start.2 = ((bf16[16,256,128]{2,1,0:T(8,128)(2,1)}), bf16[16,256,128]{2,1,0:T(8,128)(2,1)S(1)}, u32[]{:S(2)}, u32[]{:S(2)}) async-start(bf16[16,256,128]{2,1,0:T(8,128)(2,1)} %concatenate.19), calls=%async_computation.2 | async-start | bytes 2097152 | tf_op jit(solution)/shard_map/all_to_all | solution.py:63
  134.5 3.5 %copy-start.5 = (bf16[128,4096]{0,1:T(8,128)(2,1)S(1)}, bf16[128,4096]{0,1:T(8,128)(2,1)}, u32[]{:S(2)}) copy-start(bf16[128,4096]{0,1:T(8,128)(2,1)} %copy-done.4) | copy-start | bytes 3145732
  138.1 4.9 %copy-start.10 = (f32[4096]{0:T(1024)S(1)}, f32[4096]{0:T(1024)}, u32[]{:S(2)}) copy-start(f32[4096]{0:T(1024)} %param.11) | copy-start | bytes 49156
where the time goes:
time: 149 us; the launch traced here: 146 us
  waiting for transfers between devices  66.8 us (45%)
  local copies, waits for them, and re-layouts  28.5 us (19%)
  starting transfers between devices  22.8 us (15%)
  other arithmetic  17.8 us (12%)
  matrix products  10.2 us (7%)
    all_to_all x1, waiting for transfers between devices, on_device(): lax.all_to_all(stacked, 'ctx', split_axis=1, concat_axis=0, tiled=True)  43.9 us
    all_to_all x1, waiting for transfers between devices, on_device(): lax.all_to_all(shared.astype(jnp.bfloat16), 'ctx', split_axis=0, concat_a...  22.8 us
    pad x4, local copies, waits for them, and re-layouts, block_prefix(): carried = lax.associative_scan(join_rows, (rates, states), axis=0)  12.2 us
    all_to_all x1, starting transfers between devices, on_device(): lax.all_to_all(shared.astype(jnp.bfloat16), 'ctx', split_axis=0, concat_a...  8.2 us
    all_to_all x1, starting transfers between devices, on_device(): lax.all_to_all(stacked, 'ctx', split_axis=1, concat_axis=0, tiled=True)  6.03 us
    unnamed x25, local copies, waits for them, and re-layouts  5.27 us
    dot_general x1, matrix products, on_device(): jnp.einsum('hts,shd->thd', weights, value_heads, preferred_element_type=j...  4.9 us
    add x3, other arithmetic, block_prefix(): carried = lax.associative_scan(join_rows, (rates, states), axis=0)  4.9 us
  transfers between devices with their start and end apart: 4, of which 2 were waited for; matrix products, arithmetic and copies ran while one was open for 7% of the time, Pallas kernels for 0%

commit v1 on v0

v1 whole, which is shorter than its diff:
```python
import functools

import jax
import jax.numpy as jnp
from jax import lax
from jax.experimental import pallas as pl
from jax.experimental.pallas import tpu as pltpu
from jax.sharding import PartitionSpec as P

MESH = pl.DeviceIdType.MESH
F32 = jnp.float32
BF16 = jnp.bfloat16
PLANE = 4
GROUP = 4
TAIL = 16


def dot(a, b, contract, precision=None):
    return lax.dot_general(
        a, b, (contract, ((), ())), preferred_element_type=F32, precision=precision
    )


def kernel(
    n, q_hbm, k_hbm, v_hbm, ld_ref, w_ref, g_ref, out_hbm,
    q_s, k_s, v_s, out_s, halo, kx, kc_s, intra_s, cum_c, cum_t, dec, coef,
    s_all, s_low, x_recv, s_chip, y_send, y_recv, z_send, z_recv, b_send, pre,
    in_sem, halo_sem, dec_send_sem, dec_recv_sem, x_sem, y_sem, z_sem, b_sem, out_sem,
):
    rows, width = q_s.shape
    heads = ld_ref.shape[1]
    size = width // heads
    chunks = heads // GROUP
    taps = w_ref.shape[0]
    cols = GROUP * size
    planes = n // PLANE

    me = lax.axis_index("ctx")
    r = lax.rem(me, PLANE)
    z = lax.div(me, PLANE)
    core = lax.rem(me, 2)
    y = lax.div(r, 2)
    sibling = me + 1 - 2 * core
    across = me + 2 - 4 * y
    has_before = z > 0
    has_after = z < planes - 1

    k_in = pltpu.make_async_copy(k_hbm, k_s, in_sem.at[0])
    v_in = pltpu.make_async_copy(v_hbm, v_s, in_sem.at[1])
    q_in = pltpu.make_async_copy(q_hbm, q_s, in_sem.at[2])
    k_in.start()
    v_in.start()
    q_in.start()

    barrier = pltpu.get_barrier_semaphore()

    def greet(target):
        pl.semaphore_signal(barrier, inc=1, device_id={"ctx": target}, device_id_type=MESH)

    for off in range(1, PLANE):
        greet(z * PLANE + lax.rem(r + off, PLANE))
    links = (
        (has_before, me - PLANE),
        (has_after, me + PLANE),
        (jnp.logical_and(has_before, r == 0), me - 1),
        (jnp.logical_and(has_after, r == PLANE - 1), me + 1),
    )
    for there, target in links:
        @pl.when(there)
        def _(target=target):
            greet(target)

    t_at = lax.broadcasted_iota(jnp.int32, (rows, rows), 0)
    s_at = lax.broadcasted_iota(jnp.int32, (rows, rows), 1)
    lower = jnp.where(s_at <= t_at, 1.0, 0.0).astype(F32)
    upper = jnp.where(t_at <= s_at, 1.0, 0.0).astype(F32)
    log_decay = ld_ref[...]
    cum = dot(lower, log_decay, ((1,), (0,)), lax.Precision.HIGHEST)
    for c in range(chunks):
        cum_c[c, :, 0:GROUP] = cum[:, c * GROUP : (c + 1) * GROUP]
    cum_rows = dot(log_decay, upper, ((0,), (0,)), lax.Precision.HIGHEST)
    cum_t[...] = cum_rows
    dec[r] = jnp.broadcast_to(jnp.exp(cum_rows[:, rows - 1 : rows]), (heads, size))

    guests = PLANE - 1
    for there, _ in links:
        guests = guests + jnp.where(there, 1, 0)
    pl.semaphore_wait(barrier, guests)

    def halo_copy(target):
        return pltpu.make_async_remote_copy(
            src_ref=k_hbm.at[pl.ds(rows - TAIL, TAIL), :],
            dst_ref=halo,
            send_sem=halo_sem.at[0],
            recv_sem=halo_sem.at[1],
            device_id={"ctx": target},
            device_id_type=MESH,
        )

    @pl.when(me < n - 1)
    def _():
        halo_copy(me + 1).start()

    def dec_copy(off, slot):
        return pltpu.make_async_remote_copy(
            src_ref=dec.at[slot],
            dst_ref=dec.at[slot],
            send_sem=dec_send_sem.at[off - 1],
            recv_sem=dec_recv_sem.at[off - 1],
            device_id={"ctx": z * PLANE + lax.rem(r + off, PLANE)},
            device_id_type=MESH,
        )

    for off in range(1, PLANE):
        dec_copy(off, r).start()

    def x_copy(j):
        return pltpu.make_async_remote_copy(
            src_ref=s_low.at[j, pl.ds(2 * (1 - core), 2)],
            dst_ref=x_recv.at[j],
            send_sem=x_sem.at[0, j],
            recv_sem=x_sem.at[1, j],
            device_id={"ctx": sibling},
            device_id_type=MESH,
        )

    def y_copy(j):
        return pltpu.make_async_remote_copy(
            src_ref=y_send.at[j],
            dst_ref=y_recv.at[j],
            send_sem=y_sem.at[0, j],
            recv_sem=y_sem.at[1, j],
            device_id={"ctx": across},
            device_id_type=MESH,
        )

    def z_copy(j):
        return pltpu.make_async_remote_copy(
            src_ref=z_send.at[j],
            dst_ref=z_recv.at[j],
            send_sem=z_sem.at[0, j],
            recv_sem=z_sem.at[1, j],
            device_id={"ctx": me + PLANE},
            device_id_type=MESH,
        )

    def b_copy(j, owner):
        return pltpu.make_async_remote_copy(
            src_ref=b_send.at[j],
            dst_ref=pre.at[j, pl.ds(2 * owner, 2)],
            send_sem=b_sem.at[0, j],
            recv_sem=b_sem.at[1, j],
            device_id={"ctx": sibling},
            device_id_type=MESH,
        )

    def out_copy(j):
        here = pl.ds(pl.multiple_of(j * cols, cols), cols)
        return pltpu.make_async_copy(out_s.at[:, here], out_hbm.at[:, here], out_sem.at[j])

    @pl.when(jnp.logical_not(has_before))
    def _():
        z_recv[...] = jnp.zeros_like(z_recv)

    k_in.wait()
    v_in.wait()

    @pl.when(me == 0)
    def _():
        halo[...] = jnp.zeros_like(halo)

    @pl.when(me > 0)
    def _():
        halo_copy(me).wait_recv()

    def head_columns(j, i):
        return pl.ds(pl.multiple_of(j * cols + i * size, size), size)

    def states(j):
        wide = pl.ds(pl.multiple_of(j * cols, cols), cols)
        kx[0:8, :] = halo[:, wide].astype(F32)[TAIL - 8 : TAIL]
        kx[pl.ds(8, rows), :] = k_s[:, wide].astype(F32)
        cum_j = cum_c[j][:, 0:GROUP]
        fade = jnp.exp(cum_j[rows - 1 : rows, :] - cum_j)
        for i in range(GROUP):
            at = head_columns(j, i)
            near = slice(i * size, (i + 1) * size)
            total = w_ref[0:1, at] * kx[pl.ds(8, rows), near]
            for tap in range(1, taps):
                total = total + w_ref[tap : tap + 1, at] * kx[pl.ds(8 - tap, rows), near]
            conv = total.astype(BF16)
            kc_s[:, at] = conv
            weighted = (conv.astype(F32) * fade[:, i : i + 1]).astype(BF16)
            state = dot(weighted, v_s[:, at], ((0,), (0,)))
            s_all[j, i] = state
            s_low[j, i] = state.astype(BF16)

    def ordered(flag, mine, other):
        return jnp.where(flag, mine, other), jnp.where(flag, other, mine)

    def chip_states(j):
        for a in range(2):
            h = j * GROUP + 2 * core + a
            first, second = ordered(core == 0, s_all[j, 2 * core + a], x_recv[j, a].astype(F32))
            joined = dec[2 * y + 1, pl.ds(h, 1), :] * first + second
            s_chip[j, a] = joined
            y_send[j, a] = joined.astype(BF16)

    def state_step(j, carry):
        @pl.when(j < chunks)
        def _():
            states(j)
            x_copy(j).start()

        @pl.when(j == 0)
        def _():
            for off in range(1, PLANE):
                dec_copy(off, lax.rem(r - off + PLANE, PLANE)).wait_recv()
            coef[0] = dec[0] * dec[1]
            coef[1] = dec[2] * dec[3]
            coef[2] = dec[0] * dec[1] * (dec[2] * dec[3])

        @pl.when(j > 0)
        def _():
            x_copy(j - 1).wait_recv()
            chip_states(j - 1)
            y_copy(j - 1).start()

        return carry

    lax.fori_loop(0, chunks + 1, state_step, 0)
    q_in.wait()

    def within(j):
        cum_j = cum_c[j][:, 0:GROUP]
        for i in range(GROUP):
            at = head_columns(j, i)
            scores = dot(q_s[:, at], kc_s[:, at], ((1,), (1,)))
            spread = cum_j[:, i : i + 1] - cum_t[pl.ds(j * GROUP + i, 1), :]
            ratio = jnp.exp(jnp.where(s_at <= t_at, spread, -1e30))
            weights = (scores * ratio).astype(BF16)
            intra_s[:, at] = dot(weights, v_s[:, at], ((1,), (0,)))

    def prefixes(j):
        for a in range(2):
            h = pl.ds(j * GROUP + 2 * core + a, 1)
            first, second = ordered(y == 0, s_chip[j, a], y_recv[j, a].astype(F32))
            before = z_recv[j, a].astype(F32)
            plane = coef[1, h, :] * first + second
            z_send[j, a] = (coef[2, h, :] * before + plane).astype(BF16)
            base = jnp.where(y == 0, before, coef[0, h, :] * before + first)
            chip_first = jnp.where(core == 0, s_all[j, 2 * core + a], x_recv[j, a].astype(F32))
            next_base = dec[2 * y, h, :] * base + chip_first
            mine, other = ordered(core == 0, base, next_base)
            pre[j, 2 * core + a] = mine.astype(BF16)
            b_send[j, a] = other.astype(BF16)

    def finish(j):
        grow = jnp.exp(cum_c[j][:, 0:GROUP])
        for i in range(GROUP):
            at = head_columns(j, i)
            inter = dot(q_s[:, at], pre[j, i], ((1,), (0,)))
            mixed = intra_s[:, at] + inter * grow[:, i : i + 1]
            mean = jnp.mean(mixed * mixed, axis=1, keepdims=True)
            out_s[:, at] = (mixed * lax.rsqrt(mean + 1e-05) * g_ref[:, at]).astype(BF16)

    def prefix_step(j, carry):
        @pl.when(j < chunks)
        def _():
            within(j)
            y_copy(j).wait_recv()

            @pl.when(has_before)
            def _():
                z_copy(j).wait_recv()

            prefixes(j)

            @pl.when(has_after)
            def _():
                z_copy(j).start()

            b_copy(j, core).start()

        @pl.when(j > 0)
        def _():
            b_copy(j - 1, 1 - core).wait_recv()
            finish(j - 1)
            out_copy(j - 1).start()

        return carry

    lax.fori_loop(0, chunks + 1, prefix_step, 0)

    def drain(j, carry):
        x_copy(j).wait_send()
        y_copy(j).wait_send()
        b_copy(j, core).wait_send()

        @pl.when(has_after)
        def _():
            z_copy(j).wait_send()

        out_copy(j).wait()
        return carry

    lax.fori_loop(0, chunks, drain, 0)
    for off in range(1, PLANE):
        dec_copy(off, r).wait_send()

    @pl.when(me < n - 1)
    def _():
        halo_copy(me + 1).wait_send()


def on_device(n, queries, key_input, value_input, log_decay, conv_weight, norm_gain):
    rows, width = queries.shape
    heads = log_decay.shape[1]
    size = width // heads
    chunks = heads // GROUP
    pair = pltpu.VMEM((chunks, 2, size, size), BF16)
    pair_wide = pltpu.VMEM((chunks, 2, size, size), F32)
    hbm = pl.BlockSpec(memory_space=pl.ANY)
    vmem = pl.BlockSpec(memory_space=pltpu.VMEM)
    dma = pltpu.SemaphoreType.DMA
    block = pltpu.VMEM((rows, width), BF16)
    return pl.pallas_call(
        functools.partial(kernel, n),
        out_shape=jax.ShapeDtypeStruct((rows, width), BF16),
        in_specs=[hbm, hbm, hbm, vmem, vmem, vmem],
        out_specs=hbm,
        scratch_shapes=[
            block, block, block, block,
            pltpu.VMEM((TAIL, width), BF16),
            pltpu.VMEM((rows + 8, GROUP * size), F32),
            block,
            pltpu.VMEM((rows, width), F32),
            pltpu.VMEM((chunks, rows, size), F32),
            pltpu.VMEM((heads, rows), F32),
            pltpu.VMEM((PLANE, heads, size), F32),
            pltpu.VMEM((3, heads, size), F32),
            pltpu.VMEM((chunks, GROUP, size, size), F32),
            pltpu.VMEM((chunks, GROUP, size, size), BF16),
            pair, pair_wide, pair, pair, pair, pair, pair,
            pltpu.VMEM((chunks, GROUP, size, size), BF16),
            dma((3,)), dma((2,)), dma((PLANE - 1,)), dma((PLANE - 1,)),
            dma((2, chunks)), dma((2, chunks)), dma((2, chunks)), dma((2, chunks)),
            dma((chunks,)),
        ],
        compiler_params=pltpu.CompilerParams(
            collective_id=0, has_side_effects=True, vmem_limit_bytes=40 * 1024 * 1024
        ),
        name="decayed_attention",
    )(queries, key_input, value_input, log_decay, conv_weight, norm_gain.reshape(1, width))


def solution(mesh):
    rows = P(("groups", "ctx"), None)
    return jax.shard_map(
        functools.partial(on_device, mesh.shape["ctx"]),
        mesh=mesh,
        in_specs=(rows, rows, rows, rows, P(), P()),
        out_specs=rows,
        check_vma=False,
    )
```

time: 149 us -> 39.4 us (0.26); the launches traced: 146 us -> 38.9 us
  waiting for transfers between devices: 66.8 us -> 0 us
  Pallas kernels: 0 us -> 33.3 us
  local copies, waits for them, and re-layouts: 28.5 us -> 5.49 us
  starting transfers between devices: 22.8 us -> 0 us
  other arithmetic: 17.8 us -> 0 us
  matrix products: 10.2 us -> 0 us
    all_to_all x3 -> x0, waiting for transfers between devices: 66.8 us -> none  [the longest x1 43.9 us: on_device(): lax.all_to_all(stacked, 'ctx', split_axis=1, concat_axis=0, tiled=True)]
    pallas_call x0 -> x1, Pallas kernels: none -> 33.3 us  [on_device(): pl.pallas_call(functools.partial(kernel, n), out_shape=jax.ShapeDtypeStru...]
    all_to_all x3 -> x0, starting transfers between devices: 19.1 us -> none  [the longest x1 8.2 us: on_device(): lax.all_to_all(shared.astype(jnp.bfloat16), 'ctx', split_axis=0, concat_a...]
    pad x4 -> x0, local copies, waits for them, and re-layouts: 12.2 us -> none  [block_prefix(): carried = lax.associative_scan(join_rows, (rates, states), axis=0)]
    dot_general x3 -> x0, matrix products: 10.2 us -> none  [the longest x1 4.9 us: on_device(): jnp.einsum('hts,shd->thd', weights, value_heads, preferred_element_type=j...]
    add x8 -> x0, other arithmetic: 7.34 us -> none  [the longest x3 4.9 us: block_prefix(): carried = lax.associative_scan(join_rows, (rates, states), axis=0)]
    slice x15 -> x0, local copies, waits for them, and re-layouts: 6.96 us -> none  [the longest x1 4.02 us: block_prefix(): return jnp.concatenate([jnp.zeros_like(inclusive[:1]), inclusive[:-1]], 0)]
    convert_element_type x2 -> x0, other arithmetic: 5.95 us -> none  [the longest x1 4.01 us: on_device(): conv_sum.astype(jnp.bfloat16).reshape(row_count, head_count, head_size)]
  transfers between devices with their start and end apart: 4 -> 0, of which waited for: 2 -> 0; matrix products, arithmetic and copies ran while one was open for 7% -> 0% of each run, Pallas kernels for 0% -> 0%
where the time goes in v1:
time: 39.4 us; the launch traced here: 38.9 us
  Pallas kernels  33.3 us (85%)
  local copies, waits for them, and re-layouts  5.49 us (14%)
    pallas_call x1, Pallas kernels, on_device(): pl.pallas_call(functools.partial(kernel, n), out_shape=jax.ShapeDtypeStru...  33.3 us
    unnamed x12, local copies, waits for them, and re-layouts  5.49 us

profile of v1, /device:TPU:27, one launch (start us, length us, event | category | flops | bytes accessed | tf_op | source)
XLA Modules:
  0.0 38.9 jit_solution(17171924064460686728)
XLA Ops:
  0.0 0.0 copy-start.3
  0.0 0.0 copy-start.4
  0.0 0.8 %copy.7.ld_ref = f32[128,32]{1,0:T(8,128)S(1)} copy(f32[128,32]{0,1:T(8,128)} %param.9) | data formatting | bytes 32768 | tf_op args[3]
  0.8 0.0 copy-done.3
  0.9 0.0 copy-done.4
  0.9 0.0 copy-start
  0.9 1.2 %copy-done = bf16[128,4096]{1,0:T(8,128)(2,1)S(1)} copy-done((bf16[128,4096]{1,0:T(8,128)(2,1)S(1)}, bf16[128,4096]{1,0:T(8,128)(2,1)}, u32[]{:S(2)}) %copy-start) | copy-done | bytes 1048600
  2.1 0.0 copy-start.1
  2.1 1.2 %copy-done.1 = bf16[128,4096]{1,0:T(8,128)(2,1)S(1)} copy-done((bf16[128,4096]{1,0:T(8,128)(2,1)S(1)}, bf16[128,4096]{1,0:T(8,128)(2,1)}, u32[]{:S(2)}) %copy-start.1) | copy-done | bytes 1048600
  3.3 0.0 copy-start.2
  3.3 1.2 %copy-done.2 = bf16[128,4096]{1,0:T(8,128)(2,1)S(1)} copy-done((bf16[128,4096]{1,0:T(8,128)(2,1)S(1)}, bf16[128,4096]{1,0:T(8,128)(2,1)}, u32[]{:S(2)}) %copy-start.2) | copy-done | bytes 1048600
  4.5 33.3 %decayed_attention.1 = bf16[128,4096]{1,0:T(8,128)(2,1)S(1)} custom-call(bf16[128,4096]{1,0:T(8,128)(2,1)S(1)} %copy-done, bf16[128,4096]{1,0:T(8,128)(2,1)S(1)} %copy-done.1, bf16[128,4096]{1,0:T(8,128)(2,1)S(1)} %copy-done.2, f32[128,32]{1,0:T(8,128)S(1)} %copy.7.ld_ref, f32[4,4096]{1,0:T(4,128)S(1)} %copy-done.3, f32[1,4096]{1,0:T(1,128)S(1)} %bitcast.1), custom_call_target="tpu_custom_call" | custom-call | tf_op jit(solution)/shard_map/decayed_attention/pallas_call | solution.py:327
  37.9 1.0 %copy.9 = bf16[128,4096]{1,0:T(8,128)(2,1)} copy(bf16[128,4096]{1,0:T(8,128)(2,1)S(1)} %decayed_attention.1) | data formatting | bytes 2097152
Async XLA Ops:
  0.0 0.9 %copy-start.3 = (f32[4,4096]{1,0:T(4,128)S(1)}, f32[4,4096]{1,0:T(4,128)}, u32[]{:S(2)}) copy-start(f32[4,4096]{1,0:T(4,128)} %w_ref.1) | copy-start | bytes 196612
  0.0 0.9 %copy-start.4 = (f32[4096]{0:T(1024)S(1)}, f32[4096]{0:T(1024)}, u32[]{:S(2)}) copy-start(f32[4096]{0:T(1024)} %param.11) | copy-start | bytes 49156
  0.9 1.2 %copy-start = (bf16[128,4096]{1,0:T(8,128)(2,1)S(1)}, bf16[128,4096]{1,0:T(8,128)(2,1)}, u32[]{:S(2)}) copy-start(bf16[128,4096]{1,0:T(8,128)(2,1)} %q_hbm.1) | copy-start | bytes 3145732
  2.1 1.2 %copy-start.1 = (bf16[128,4096]{1,0:T(8,128)(2,1)S(1)}, bf16[128,4096]{1,0:T(8,128)(2,1)}, u32[]{:S(2)}) copy-start(bf16[128,4096]{1,0:T(8,128)(2,1)} %k_hbm.1) | copy-start | bytes 3145732
  3.3 1.2 %copy-start.2 = (bf16[128,4096]{1,0:T(8,128)(2,1)S(1)}, bf16[128,4096]{1,0:T(8,128)(2,1)}, u32[]{:S(2)}) copy-start(bf16[128,4096]{1,0:T(8,128)(2,1)} %v_hbm.1) | copy-start | bytes 3145732

commit v2 on v1

--- a/solution.py
+++ b/solution.py
@@ -25,10 +25,10 @@
     n, q_hbm, k_hbm, v_hbm, ld_ref, w_ref, g_ref, out_hbm,
     q_s, k_s, v_s, out_s, halo, kx, kc_s, intra_s, cum_c, cum_t, dec, coef,
     s_all, s_low, x_recv, s_chip, y_send, y_recv, z_send, z_recv, b_send, pre,
-    in_sem, halo_sem, dec_send_sem, dec_recv_sem, x_sem, y_sem, z_sem, b_sem, out_sem,
+    in_sem, q_sem, halo_sem, dec_send_sem, dec_recv_sem, x_sem, y_sem, z_sem, b_sem, out_sem,
 ):
     rows, width = q_s.shape
-    heads = ld_ref.shape[1]
+    heads = ld_ref.shape[0]
     size = width // heads
     chunks = heads // GROUP
     taps = w_ref.shape[0]
@@ -45,11 +45,20 @@
     has_before = z > 0
     has_after = z < planes - 1
 
-    k_in = pltpu.make_async_copy(k_hbm, k_s, in_sem.at[0])
-    v_in = pltpu.make_async_copy(v_hbm, v_s, in_sem.at[1])
-    q_in = pltpu.make_async_copy(q_hbm, q_s, in_sem.at[2])
-    k_in.start()
-    v_in.start()
+    def chunk_columns(j):
+        return pl.ds(pl.multiple_of(j * cols, cols), cols)
+
+    def load(source, target, kind, j):
+        here = chunk_columns(j)
+        return pltpu.make_async_copy(source.at[:, here], target.at[:, here], in_sem.at[kind, j])
+
+    def start_loads(j, carry):
+        load(k_hbm, k_s, 0, j).start()
+        load(v_hbm, v_s, 1, j).start()
+        return carry
+
+    lax.fori_loop(0, chunks, start_loads, 0)
+    q_in = pltpu.make_async_copy(q_hbm, q_s, q_sem)
     q_in.start()
 
     barrier = pltpu.get_barrier_semaphore()
@@ -75,10 +84,10 @@
     lower = jnp.where(s_at <= t_at, 1.0, 0.0).astype(F32)
     upper = jnp.where(t_at <= s_at, 1.0, 0.0).astype(F32)
     log_decay = ld_ref[...]
-    cum = dot(lower, log_decay, ((1,), (0,)), lax.Precision.HIGHEST)
+    cum = dot(lower, log_decay, ((1,), (1,)), lax.Precision.HIGHEST)
     for c in range(chunks):
         cum_c[c, :, 0:GROUP] = cum[:, c * GROUP : (c + 1) * GROUP]
-    cum_rows = dot(log_decay, upper, ((0,), (0,)), lax.Precision.HIGHEST)
+    cum_rows = dot(log_decay, upper, ((1,), (0,)), lax.Precision.HIGHEST)
     cum_t[...] = cum_rows
     dec[r] = jnp.broadcast_to(jnp.exp(cum_rows[:, rows - 1 : rows]), (heads, size))
 
@@ -155,15 +164,12 @@
         )
 
     def out_copy(j):
-        here = pl.ds(pl.multiple_of(j * cols, cols), cols)
+        here = chunk_columns(j)
         return pltpu.make_async_copy(out_s.at[:, here], out_hbm.at[:, here], out_sem.at[j])
 
     @pl.when(jnp.logical_not(has_before))
     def _():
         z_recv[...] = jnp.zeros_like(z_recv)
-
-    k_in.wait()
-    v_in.wait()
 
     @pl.when(me == 0)
     def _():
@@ -177,7 +183,9 @@
         return pl.ds(pl.multiple_of(j * cols + i * size, size), size)
 
     def states(j):
-        wide = pl.ds(pl.multiple_of(j * cols, cols), cols)
+        load(k_hbm, k_s, 0, j).wait()
+        load(v_hbm, v_s, 1, j).wait()
+        wide = chunk_columns(j)
         kx[0:8, :] = halo[:, wide].astype(F32)[TAIL - 8 : TAIL]
         kx[pl.ds(8, rows), :] = k_s[:, wide].astype(F32)
         cum_j = cum_c[j][:, 0:GROUP]
@@ -206,31 +214,6 @@
             s_chip[j, a] = joined
             y_send[j, a] = joined.astype(BF16)
 
-    def state_step(j, carry):
-        @pl.when(j < chunks)
-        def _():
-            states(j)
-            x_copy(j).start()
-
-        @pl.when(j == 0)
-        def _():
-            for off in range(1, PLANE):
-                dec_copy(off, lax.rem(r - off + PLANE, PLANE)).wait_recv()
-            coef[0] = dec[0] * dec[1]
-            coef[1] = dec[2] * dec[3]
-            coef[2] = dec[0] * dec[1] * (dec[2] * dec[3])
-
-        @pl.when(j > 0)
-        def _():
-            x_copy(j - 1).wait_recv()
-            chip_states(j - 1)
-            y_copy(j - 1).start()
-
-        return carry
-
-    lax.fori_loop(0, chunks + 1, state_step, 0)
-    q_in.wait()
-
     def within(j):
         cum_j = cum_c[j][:, 0:GROUP]
         for i in range(GROUP):
@@ -264,33 +247,71 @@
             mean = jnp.mean(mixed * mixed, axis=1, keepdims=True)
             out_s[:, at] = (mixed * lax.rsqrt(mean + 1e-05) * g_ref[:, at]).astype(BF16)
 
-    def prefix_step(j, carry):
-        @pl.when(j < chunks)
-        def _():
-            within(j)
-            y_copy(j).wait_recv()
-
-            @pl.when(has_before)
-            def _():
-                z_copy(j).wait_recv()
-
-            prefixes(j)
-
-            @pl.when(has_after)
-            def _():
-                z_copy(j).start()
-
-            b_copy(j, core).start()
-
-        @pl.when(j > 0)
-        def _():
-            b_copy(j - 1, 1 - core).wait_recv()
-            finish(j - 1)
-            out_copy(j - 1).start()
-
+    chain_lag = jnp.minimum(2 + 3 * z, chunks + 3)
+    within_lag = chunks
+    finish_lag = jnp.maximum(chain_lag + 2, within_lag + 1)
+
+    def during(step, lag, work):
+        j = step - lag
+
+        @pl.when(jnp.logical_and(j >= 0, j < chunks))
+        def _():
+            work(j)
+
+    def state_part(j):
+        states(j)
+        x_copy(j).start()
+
+    def chip_part(j):
+        x_copy(j).wait_recv()
+        chip_states(j)
+        y_copy(j).start()
+
+    def chain_part(j):
+        y_copy(j).wait_recv()
+
+        @pl.when(has_before)
+        def _():
+            z_copy(j).wait_recv()
+
+        prefixes(j)
+
+        @pl.when(has_after)
+        def _():
+            z_copy(j).start()
+
+        b_copy(j, core).start()
+
+    def within_part(j):
+        @pl.when(j == 0)
+        def _():
+            q_in.wait()
+
+        within(j)
+
+    def finish_part(j):
+        b_copy(j, 1 - core).wait_recv()
+        finish(j)
+        out_copy(j).start()
+
+    def one_step(step, carry):
+        during(step, 0, state_part)
+
+        @pl.when(step == 0)
+        def _():
+            for off in range(1, PLANE):
+                dec_copy(off, lax.rem(r - off + PLANE, PLANE)).wait_recv()
+            coef[0] = dec[0] * dec[1]
+            coef[1] = dec[2] * dec[3]
+            coef[2] = dec[0] * dec[1] * (dec[2] * dec[3])
+
+        during(step, 1, chip_part)
+        during(step, chain_lag, chain_part)
+        during(step, within_lag, within_part)
+        during(step, finish_lag, finish_part)
         return carry
 
-    lax.fori_loop(0, chunks + 1, prefix_step, 0)
+    lax.fori_loop(0, 2 * chunks + 5, one_step, 0)
 
     def drain(j, carry):
         x_copy(j).wait_send()
@@ -343,15 +364,15 @@
             pltpu.VMEM((chunks, GROUP, size, size), BF16),
             pair, pair_wide, pair, pair, pair, pair, pair,
             pltpu.VMEM((chunks, GROUP, size, size), BF16),
-            dma((3,)), dma((2,)), dma((PLANE - 1,)), dma((PLANE - 1,)),
+            dma((2, chunks)), dma, dma((2,)), dma((PLANE - 1,)), dma((PLANE - 1,)),
             dma((2, chunks)), dma((2, chunks)), dma((2, chunks)), dma((2, chunks)),
             dma((chunks,)),
         ],
         compiler_params=pltpu.CompilerParams(
-            collective_id=0, has_side_effects=True, vmem_limit_bytes=40 * 1024 * 1024
+            collective_id=0, has_side_effects=True, vmem_limit_bytes=60 * 1024 * 1024
         ),
         name="decayed_attention",
-    )(queries, key_input, value_input, log_decay, conv_weight, norm_gain.reshape(1, width))
+    )(queries, key_input, value_input, log_decay.T, conv_weight, norm_gain.reshape(1, width))
 
 
 def solution(mesh):

time: 39.4 us -> 39.3 us (level)
  local copies, waits for them, and re-layouts: 5.49 us -> 2.29 us
  Pallas kernels: 33.3 us -> 36.3 us
    unnamed x12 -> x1, local copies, waits for them, and re-layouts: 5.49 us -> 2.29 us
    pallas_call x1, Pallas kernels: 33.3 us -> 36.3 us  [on_device(): pl.pallas_call(functools.partial(kernel, n), out_shape=jax.ShapeDtypeStru...]
where the time goes in v2:
time: 39.3 us; the launch traced here: 38.6 us
  Pallas kernels  36.3 us (92%)
  local copies, waits for them, and re-layouts  2.29 us (6%)
    pallas_call x1, Pallas kernels, on_device(): pl.pallas_call(functools.partial(kernel, n), out_shape=jax.ShapeDtypeStru...  36.3 us
    unnamed x1, local copies, waits for them, and re-layouts  2.29 us

profile of v2, /device:TPU:27, one launch (start us, length us, event | category | flops | bytes accessed | tf_op | source)
XLA Modules:
  0.0 38.6 jit_solution(10749823887955021168)
XLA Ops:
  0.0 36.3 %decayed_attention.1 = bf16[128,4096]{1,0:T(8,128)(2,1)} custom-call(bf16[128,4096]{1,0:T(8,128)(2,1)} %q_hbm.1, bf16[128,4096]{1,0:T(8,128)(2,1)} %k_hbm.1, bf16[128,4096]{1,0:T(8,128)(2,1)} %v_hbm.1, f32[32,128]{1,0:T(8,128)} %bitcast.2, f32[4,4096]{1,0:T(4,128)} %w_ref.1, f32[1,4096]{1,0:T(1,128)} %bitcast.3), custom_call_target="tpu_custom_call" | custom-call | tf_op jit(solution)/shard_map/decayed_attention/pallas_call | solution.py:348
  36.3 2.3 %copy.8 = bf16[128,4096]{1,0:T(8,128)(2,1)} copy(bf16[128,4096]{1,0:T(8,128)(2,1)} %decayed_attention.1) | data formatting | bytes 2097152

commit v3 on v2

--- a/solution.py
+++ b/solution.py
@@ -13,6 +13,7 @@
 PLANE = 4
 GROUP = 4
 TAIL = 16
+PARTS = 4
 
 
 def dot(a, b, contract, precision=None):
@@ -23,9 +24,9 @@
 
 def kernel(
     n, q_hbm, k_hbm, v_hbm, ld_ref, w_ref, g_ref, out_hbm,
-    q_s, k_s, v_s, out_s, halo, kx, kc_s, intra_s, cum_c, cum_t, dec, coef,
+    q_s, k_s, v_s, out_s, tail, tail_out, tail_in, halo, kx, kc_s, intra_s, cum_c, cum_t, fade_t, dec, coef,
     s_all, s_low, x_recv, s_chip, y_send, y_recv, z_send, z_recv, b_send, pre,
-    in_sem, q_sem, halo_sem, dec_send_sem, dec_recv_sem, x_sem, y_sem, z_sem, b_sem, out_sem,
+    in_sem, q_sem, tail_sem, halo_sem, dec_send_sem, dec_recv_sem, x_sem, y_sem, z_sem, b_sem, out_sem,
 ):
     rows, width = q_s.shape
     heads = ld_ref.shape[0]
@@ -51,6 +52,9 @@
     def load(source, target, kind, j):
         here = chunk_columns(j)
         return pltpu.make_async_copy(source.at[:, here], target.at[:, here], in_sem.at[kind, j])
+
+    tail_load = pltpu.make_async_copy(k_hbm.at[pl.ds(rows - TAIL, TAIL), :], tail, tail_sem)
+    tail_load.start()
 
     def start_loads(j, carry):
         load(k_hbm, k_s, 0, j).start()
@@ -91,6 +95,15 @@
     cum_t[...] = cum_rows
     dec[r] = jnp.broadcast_to(jnp.exp(cum_rows[:, rows - 1 : rows]), (heads, size))
 
+    fade_t[...] = jnp.exp(cum_rows[:, rows - 1 : rows] - cum_rows)
+    keep = taps - 1
+    part = width // PARTS
+    tail_load.wait()
+    last = tail[...].astype(F32)[TAIL - keep : TAIL]
+    packed = [last[:, p * part : (p + 1) * part] for p in range(PARTS)]
+    packed.append(jnp.zeros((TAIL - PARTS * keep, part), F32))
+    tail_out[...] = jnp.concatenate(packed, axis=0).astype(BF16)
+
     guests = PLANE - 1
     for there, _ in links:
         guests = guests + jnp.where(there, 1, 0)
@@ -98,8 +111,8 @@
 
     def halo_copy(target):
         return pltpu.make_async_remote_copy(
-            src_ref=k_hbm.at[pl.ds(rows - TAIL, TAIL), :],
-            dst_ref=halo,
+            src_ref=tail_out,
+            dst_ref=tail_in,
             send_sem=halo_sem.at[0],
             recv_sem=halo_sem.at[1],
             device_id={"ctx": target},
@@ -178,6 +191,9 @@
     @pl.when(me > 0)
     def _():
         halo_copy(me).wait_recv()
+        got = tail_in[...].astype(F32)
+        for p in range(PARTS):
+            halo[8 - keep : 8, p * part : (p + 1) * part] = got[p * keep : (p + 1) * keep]
 
     def head_columns(j, i):
         return pl.ds(pl.multiple_of(j * cols + i * size, size), size)
@@ -186,22 +202,24 @@
         load(k_hbm, k_s, 0, j).wait()
         load(v_hbm, v_s, 1, j).wait()
         wide = chunk_columns(j)
-        kx[0:8, :] = halo[:, wide].astype(F32)[TAIL - 8 : TAIL]
+        kx[0:8, :] = halo[:, wide]
         kx[pl.ds(8, rows), :] = k_s[:, wide].astype(F32)
-        cum_j = cum_c[j][:, 0:GROUP]
-        fade = jnp.exp(cum_j[rows - 1 : rows, :] - cum_j)
+        taps_j = w_ref[:, wide]
+        fade = [fade_t[pl.ds(j * GROUP + i, 1), :] for i in range(GROUP)]
+        values = [v_s[:, head_columns(j, i)] for i in range(GROUP)]
+        turned = []
         for i in range(GROUP):
-            at = head_columns(j, i)
             near = slice(i * size, (i + 1) * size)
-            total = w_ref[0:1, at] * kx[pl.ds(8, rows), near]
+            total = taps_j[0:1, near] * kx[pl.ds(8, rows), near]
             for tap in range(1, taps):
-                total = total + w_ref[tap : tap + 1, at] * kx[pl.ds(8 - tap, rows), near]
-            conv = total.astype(BF16)
-            kc_s[:, at] = conv
-            weighted = (conv.astype(F32) * fade[:, i : i + 1]).astype(BF16)
-            state = dot(weighted, v_s[:, at], ((0,), (0,)))
-            s_all[j, i] = state
-            s_low[j, i] = state.astype(BF16)
+                total = total + taps_j[tap : tap + 1, near] * kx[pl.ds(8 - tap, rows), near]
+            turned.append(total.T.astype(BF16))
+        weighted = [(turned[i].astype(F32) * fade[i]).astype(BF16) for i in range(GROUP)]
+        state = [dot(weighted[i], values[i], ((1,), (0,))) for i in range(GROUP)]
+        for i in range(GROUP):
+            kc_s[j, i] = turned[i]
+            s_all[j, i] = state[i]
+            s_low[j, i] = state[i].astype(BF16)
 
     def ordered(flag, mine, other):
         return jnp.where(flag, mine, other), jnp.where(flag, other, mine)
@@ -216,13 +234,17 @@
 
     def within(j):
         cum_j = cum_c[j][:, 0:GROUP]
-        for i in range(GROUP):
-            at = head_columns(j, i)
-            scores = dot(q_s[:, at], kc_s[:, at], ((1,), (1,)))
-            spread = cum_j[:, i : i + 1] - cum_t[pl.ds(j * GROUP + i, 1), :]
-            ratio = jnp.exp(jnp.where(s_at <= t_at, spread, -1e30))
-            weights = (scores * ratio).astype(BF16)
-            intra_s[:, at] = dot(weights, v_s[:, at], ((1,), (0,)))
+        each = range(GROUP)
+        scores = [dot(q_s[:, head_columns(j, i)], kc_s[j, i], ((1,), (0,))) for i in each]
+        values = [v_s[:, head_columns(j, i)] for i in each]
+        ahead = [cum_t[pl.ds(j * GROUP + i, 1), :] for i in each]
+        weights = []
+        for i in each:
+            spread = jnp.where(s_at <= t_at, cum_j[:, i : i + 1] - ahead[i], -1e30)
+            weights.append((scores[i] * jnp.exp(spread)).astype(BF16))
+        intra = [dot(weights[i], values[i], ((1,), (0,))) for i in each]
+        for i in each:
+            intra_s[:, head_columns(j, i)] = intra[i]
 
     def prefixes(j):
         for a in range(2):
@@ -240,15 +262,22 @@
 
     def finish(j):
         grow = jnp.exp(cum_c[j][:, 0:GROUP])
-        for i in range(GROUP):
-            at = head_columns(j, i)
-            inter = dot(q_s[:, at], pre[j, i], ((1,), (0,)))
-            mixed = intra_s[:, at] + inter * grow[:, i : i + 1]
-            mean = jnp.mean(mixed * mixed, axis=1, keepdims=True)
-            out_s[:, at] = (mixed * lax.rsqrt(mean + 1e-05) * g_ref[:, at]).astype(BF16)
-
-    chain_lag = jnp.minimum(2 + 3 * z, chunks + 3)
-    within_lag = chunks
+        gain = g_ref[:, chunk_columns(j)]
+        each = range(GROUP)
+        inter = [dot(q_s[:, head_columns(j, i)], pre[j, i], ((1,), (0,))) for i in each]
+        intra = [intra_s[:, head_columns(j, i)] for i in each]
+        mixed = [intra[i] + inter[i] * grow[:, i : i + 1] for i in each]
+        scale = [
+            lax.rsqrt(jnp.mean(mixed[i] * mixed[i], axis=1, keepdims=True) + 1e-05) for i in each
+        ]
+        result = [
+            (mixed[i] * scale[i] * gain[:, i * size : (i + 1) * size]).astype(BF16) for i in each
+        ]
+        for i in each:
+            out_s[:, head_columns(j, i)] = result[i]
+
+    chain_lag = jnp.minimum(4 + 3 * z, chunks + 4)
+    within_lag = jnp.where(z < 2, chunks, chunks // 2)
     finish_lag = jnp.maximum(chain_lag + 2, within_lag + 1)
 
     def during(step, lag, work):
@@ -311,7 +340,7 @@
         during(step, finish_lag, finish_part)
         return carry
 
-    lax.fori_loop(0, 2 * chunks + 5, one_step, 0)
+    lax.fori_loop(0, 2 * chunks + 6, one_step, 0)
 
     def drain(j, carry):
         x_copy(j).wait_send()
@@ -341,7 +370,7 @@
     chunks = heads // GROUP
     pair = pltpu.VMEM((chunks, 2, size, size), BF16)
     pair_wide = pltpu.VMEM((chunks, 2, size, size), F32)
-    hbm = pl.BlockSpec(memory_space=pl.ANY)
+    hbm = pl.BlockSpec(memory_space=pltpu.HBM)
     vmem = pl.BlockSpec(memory_space=pltpu.VMEM)
     dma = pltpu.SemaphoreType.DMA
     block = pltpu.VMEM((rows, width), BF16)
@@ -349,14 +378,18 @@
         functools.partial(kernel, n),
         out_shape=jax.ShapeDtypeStruct((rows, width), BF16),
         in_specs=[hbm, hbm, hbm, vmem, vmem, vmem],
-        out_specs=hbm,
+        out_specs=pl.BlockSpec(memory_space=pl.ANY),
         scratch_shapes=[
             block, block, block, block,
             pltpu.VMEM((TAIL, width), BF16),
+            pltpu.VMEM((TAIL, width // PARTS), BF16),
+            pltpu.VMEM((TAIL, width // PARTS), BF16),
+            pltpu.VMEM((8, width), F32),
             pltpu.VMEM((rows + 8, GROUP * size), F32),
-            block,
+            pltpu.VMEM((chunks, GROUP, size, rows), BF16),
             pltpu.VMEM((rows, width), F32),
             pltpu.VMEM((chunks, rows, size), F32),
+            pltpu.VMEM((heads, rows), F32),
             pltpu.VMEM((heads, rows), F32),
             pltpu.VMEM((PLANE, heads, size), F32),
             pltpu.VMEM((3, heads, size), F32),
@@ -364,12 +397,12 @@
             pltpu.VMEM((chunks, GROUP, size, size), BF16),
             pair, pair_wide, pair, pair, pair, pair, pair,
             pltpu.VMEM((chunks, GROUP, size, size), BF16),
-            dma((2, chunks)), dma, dma((2,)), dma((PLANE - 1,)), dma((PLANE - 1,)),
+            dma((2, chunks)), dma, dma, dma((2,)), dma((PLANE - 1,)), dma((PLANE - 1,)),
             dma((2, chunks)), dma((2, chunks)), dma((2, chunks)), dma((2, chunks)),
             dma((chunks,)),
         ],
         compiler_params=pltpu.CompilerParams(
-            collective_id=0, has_side_effects=True, vmem_limit_bytes=60 * 1024 * 1024
+            collective_id=0, has_side_effects=True, vmem_limit_bytes=52 * 1024 * 1024
         ),
         name="decayed_attention",
     )(queries, key_input, value_input, log_decay.T, conv_weight, norm_gain.reshape(1, width))

time: 39.3 us -> 33.9 us (0.86)
  Pallas kernels: 36.3 us -> 30.3 us
  local copies, waits for them, and re-layouts: 2.29 us -> 3.25 us
    pallas_call x1, Pallas kernels: 36.3 us -> 30.3 us  [on_device(): pl.pallas_call(functools.partial(kernel, n), out_shape=jax.ShapeDtypeStru...]
    unnamed x1 -> x7, local copies, waits for them, and re-layouts: 2.29 us -> 3.25 us
where the time goes in v3:
time: 33.9 us; the launch traced here: 33.5 us
  Pallas kernels  30.3 us (89%)
  local copies, waits for them, and re-layouts  3.25 us (10%)
    pallas_call x1, Pallas kernels, on_device(): pl.pallas_call(functools.partial(kernel, n), out_shape=jax.ShapeDtypeStru...  30.3 us
    unnamed x7, local copies, waits for them, and re-layouts  3.25 us

profile of v3, /device:TPU:27, one launch (start us, length us, event | category | flops | bytes accessed | tf_op | source)
XLA Modules:
  0.0 33.5 jit_solution(5645740794069239212)
XLA Ops:
  0.0 0.0 copy-start
  0.0 0.8 %copy-done = f32[4,4096]{1,0:T(4,128)S(1)} copy-done((f32[4,4096]{1,0:T(4,128)S(1)}, f32[4,4096]{1,0:T(4,128)}, u32[]{:S(2)}) %copy-start) | copy-done | bytes 65560
  0.8 0.0 copy-start.1
  0.8 0.7 %copy-done.1 = f32[128,32]{0,1:T(8,128)S(1)} copy-done((f32[128,32]{0,1:T(8,128)S(1)}, f32[128,32]{0,1:T(8,128)}, u32[]{:S(2)}) %copy-start.1) | copy-done | bytes 16408
  1.6 0.0 copy-start.2
  1.6 0.7 %copy-done.2 = f32[4096]{0:T(1024)S(1)} copy-done((f32[4096]{0:T(1024)S(1)}, f32[4096]{0:T(1024)}, u32[]{:S(2)}) %copy-start.2) | copy-done | bytes 16408
  2.3 30.3 %decayed_attention.1 = bf16[128,4096]{1,0:T(8,128)(2,1)S(1)} custom-call(bf16[128,4096]{1,0:T(8,128)(2,1)} %q_hbm.1, bf16[128,4096]{1,0:T(8,128)(2,1)} %k_hbm.1, bf16[128,4096]{1,0:T(8,128)(2,1)} %v_hbm.1, f32[32,128]{1,0:T(8,128)S(1)} %bitcast.2, f32[4,4096]{1,0:T(4,128)S(1)} %copy-done, f32[1,4096]{1,0:T(1,128)S(1)} %bitcast.3), custom_call_target="tpu_custom_call" | custom-call | tf_op jit(solution)/shard_map/decayed_attention/pallas_call | solution.py:377
  32.6 1.0 %copy.8 = bf16[128,4096]{1,0:T(8,128)(2,1)} copy(bf16[128,4096]{1,0:T(8,128)(2,1)S(1)} %decayed_attention.1) | data formatting | bytes 2097152
Async XLA Ops:
  0.0 0.8 %copy-start = (f32[4,4096]{1,0:T(4,128)S(1)}, f32[4,4096]{1,0:T(4,128)}, u32[]{:S(2)}) copy-start(f32[4,4096]{1,0:T(4,128)} %w_ref.1) | copy-start | bytes 196612
  0.8 0.7 %copy-start.1 = (f32[128,32]{0,1:T(8,128)S(1)}, f32[128,32]{0,1:T(8,128)}, u32[]{:S(2)}) copy-start(f32[128,32]{0,1:T(8,128)} %param.9) | copy-start | bytes 49156
  1.6 0.7 %copy-start.2 = (f32[4096]{0:T(1024)S(1)}, f32[4096]{0:T(1024)}, u32[]{:S(2)}) copy-start(f32[4096]{0:T(1024)} %param.11) | copy-start | bytes 49156

commit v4 on v3

--- a/solution.py
+++ b/solution.py
@@ -23,10 +23,10 @@
 
 
 def kernel(
-    n, q_hbm, k_hbm, v_hbm, ld_ref, w_ref, g_ref, out_hbm,
-    q_s, k_s, v_s, out_s, tail, tail_out, tail_in, halo, kx, kc_s, intra_s, cum_c, cum_t, fade_t, dec, coef,
-    s_all, s_low, x_recv, s_chip, y_send, y_recv, z_send, z_recv, b_send, pre,
-    in_sem, q_sem, tail_sem, halo_sem, dec_send_sem, dec_recv_sem, x_sem, y_sem, z_sem, b_sem, out_sem,
+    n, q_hbm, k_hbm, v_hbm, ld_hbm, w_hbm, g_hbm, out_hbm,
+    ld_ref, w_ref, g_ref, q_s, k_s, v_s, out_s, tail, tail_out, tail_in, halo, kx, kc_s, intra_s, cum_c, cum_t, fade_t, dec, coef,
+    s_all, s_low, x_recv, s_chip, y_send, y_recv, z_send, z_recv, r_send, base, b_send, pre,
+    in_sem, q_sem, tail_sem, small_sem, halo_sem, dec_send_sem, dec_recv_sem, x_sem, y_sem, z_sem, r_sem, b_sem, out_sem,
 ):
     rows, width = q_s.shape
     heads = ld_ref.shape[0]
@@ -53,8 +53,14 @@
         here = chunk_columns(j)
         return pltpu.make_async_copy(source.at[:, here], target.at[:, here], in_sem.at[kind, j])
 
+    small = [
+        pltpu.make_async_copy(source, target, small_sem.at[at])
+        for at, (source, target) in enumerate(((ld_hbm, ld_ref), (w_hbm, w_ref), (g_hbm, g_ref)))
+    ]
+    small[0].start()
     tail_load = pltpu.make_async_copy(k_hbm.at[pl.ds(rows - TAIL, TAIL), :], tail, tail_sem)
     tail_load.start()
+    small[1].start()
 
     def start_loads(j, carry):
         load(k_hbm, k_s, 0, j).start()
@@ -64,6 +70,7 @@
     lax.fori_loop(0, chunks, start_loads, 0)
     q_in = pltpu.make_async_copy(q_hbm, q_s, q_sem)
     q_in.start()
+    small[2].start()
 
     barrier = pltpu.get_barrier_semaphore()
 
@@ -87,6 +94,7 @@
     s_at = lax.broadcasted_iota(jnp.int32, (rows, rows), 1)
     lower = jnp.where(s_at <= t_at, 1.0, 0.0).astype(F32)
     upper = jnp.where(t_at <= s_at, 1.0, 0.0).astype(F32)
+    small[0].wait()
     log_decay = ld_ref[...]
     cum = dot(lower, log_decay, ((1,), (1,)), lax.Precision.HIGHEST)
     for c in range(chunks):
@@ -166,6 +174,16 @@
             device_id_type=MESH,
         )
 
+    def r_copy(j, owner):
+        return pltpu.make_async_remote_copy(
+            src_ref=r_send.at[j],
+            dst_ref=base.at[j, owner],
+            send_sem=r_sem.at[0, j],
+            recv_sem=r_sem.at[1, j],
+            device_id={"ctx": across},
+            device_id_type=MESH,
+        )
+
     def b_copy(j, owner):
         return pltpu.make_async_remote_copy(
             src_ref=b_send.at[j],
@@ -183,6 +201,8 @@
     @pl.when(jnp.logical_not(has_before))
     def _():
         z_recv[...] = jnp.zeros_like(z_recv)
+
+    small[1].wait()
 
     @pl.when(me == 0)
     def _():
@@ -230,7 +250,7 @@
             first, second = ordered(core == 0, s_all[j, 2 * core + a], x_recv[j, a].astype(F32))
             joined = dec[2 * y + 1, pl.ds(h, 1), :] * first + second
             s_chip[j, a] = joined
-            y_send[j, a] = joined.astype(BF16)
+        y_send[j] = s_chip[j, 1 - y].astype(BF16)
 
     def within(j):
         cum_j = cum_c[j][:, 0:GROUP]
@@ -246,17 +266,23 @@
         for i in each:
             intra_s[:, head_columns(j, i)] = intra[i]
 
+    def advance(j):
+        h = pl.ds(j * GROUP + 2 * core + y, 1)
+        first, second = ordered(y == 0, s_chip[j, y], y_recv[j].astype(F32))
+        before = z_recv[j].astype(F32)
+        plane = coef[1, h, :] * first + second
+        z_send[j] = (coef[2, h, :] * before + plane).astype(BF16)
+        mine, other = ordered(y == 0, before, coef[0, h, :] * before + first)
+        r_send[j] = other.astype(BF16)
+        base[j, y] = mine.astype(BF16)
+
     def prefixes(j):
         for a in range(2):
             h = pl.ds(j * GROUP + 2 * core + a, 1)
-            first, second = ordered(y == 0, s_chip[j, a], y_recv[j, a].astype(F32))
-            before = z_recv[j, a].astype(F32)
-            plane = coef[1, h, :] * first + second
-            z_send[j, a] = (coef[2, h, :] * before + plane).astype(BF16)
-            base = jnp.where(y == 0, before, coef[0, h, :] * before + first)
+            chip_base = base[j, a].astype(F32)
             chip_first = jnp.where(core == 0, s_all[j, 2 * core + a], x_recv[j, a].astype(F32))
-            next_base = dec[2 * y, h, :] * base + chip_first
-            mine, other = ordered(core == 0, base, next_base)
+            next_base = dec[2 * y, h, :] * chip_base + chip_first
+            mine, other = ordered(core == 0, chip_base, next_base)
             pre[j, 2 * core + a] = mine.astype(BF16)
             b_send[j, a] = other.astype(BF16)
 
@@ -276,9 +302,10 @@
         for i in each:
             out_s[:, head_columns(j, i)] = result[i]
 
-    chain_lag = jnp.minimum(4 + 3 * z, chunks + 4)
+    chain_lag = jnp.minimum(4 + lax.div(5 * z, 2), chunks + 3)
     within_lag = jnp.where(z < 2, chunks, chunks // 2)
-    finish_lag = jnp.maximum(chain_lag + 2, within_lag + 1)
+    prefix_lag = chain_lag + 3
+    finish_lag = jnp.maximum(prefix_lag + 2, within_lag + 1)
 
     def during(step, lag, work):
         j = step - lag
@@ -303,18 +330,24 @@
         def _():
             z_copy(j).wait_recv()
 
+        advance(j)
+
+        @pl.when(has_after)
+        def _():
+            z_copy(j).start()
+
+        r_copy(j, y).start()
+
+    def prefix_part(j):
+        r_copy(j, 1 - y).wait_recv()
         prefixes(j)
-
-        @pl.when(has_after)
-        def _():
-            z_copy(j).start()
-
         b_copy(j, core).start()
 
     def within_part(j):
         @pl.when(j == 0)
         def _():
             q_in.wait()
+            small[2].wait()
 
         within(j)
 
@@ -336,15 +369,17 @@
 
         during(step, 1, chip_part)
         during(step, chain_lag, chain_part)
+        during(step, prefix_lag, prefix_part)
         during(step, within_lag, within_part)
         during(step, finish_lag, finish_part)
         return carry
 
-    lax.fori_loop(0, 2 * chunks + 6, one_step, 0)
+    lax.fori_loop(0, 2 * chunks + 8, one_step, 0)
 
     def drain(j, carry):
         x_copy(j).wait_send()
         y_copy(j).wait_send()
+        r_copy(j, y).wait_send()
         b_copy(j, core).wait_send()
 
         @pl.when(has_after)
@@ -369,17 +404,23 @@
     size = width // heads
     chunks = heads // GROUP
     pair = pltpu.VMEM((chunks, 2, size, size), BF16)
+    one = pltpu.VMEM((chunks, size, size), BF16)
     pair_wide = pltpu.VMEM((chunks, 2, size, size), F32)
     hbm = pl.BlockSpec(memory_space=pltpu.HBM)
-    vmem = pl.BlockSpec(memory_space=pltpu.VMEM)
     dma = pltpu.SemaphoreType.DMA
     block = pltpu.VMEM((rows, width), BF16)
+    arguments = (
+        queries, key_input, value_input, log_decay.T, conv_weight, norm_gain.reshape(1, width)
+    )
     return pl.pallas_call(
         functools.partial(kernel, n),
         out_shape=jax.ShapeDtypeStruct((rows, width), BF16),
-        in_specs=[hbm, hbm, hbm, vmem, vmem, vmem],
+        in_specs=[hbm] * 6,
         out_specs=pl.BlockSpec(memory_space=pl.ANY),
         scratch_shapes=[
+            pltpu.VMEM((heads, rows), F32),
+            pltpu.VMEM(conv_weight.shape, F32),
+            pltpu.VMEM((1, width), F32),
             block, block, block, block,
             pltpu.VMEM((TAIL, width), BF16),
             pltpu.VMEM((TAIL, width // PARTS), BF16),
@@ -395,17 +436,17 @@
             pltpu.VMEM((3, heads, size), F32),
             pltpu.VMEM((chunks, GROUP, size, size), F32),
             pltpu.VMEM((chunks, GROUP, size, size), BF16),
-            pair, pair_wide, pair, pair, pair, pair, pair,
+            pair, pair_wide, one, one, one, one, one, pair, pair,
             pltpu.VMEM((chunks, GROUP, size, size), BF16),
-            dma((2, chunks)), dma, dma, dma((2,)), dma((PLANE - 1,)), dma((PLANE - 1,)),
-            dma((2, chunks)), dma((2, chunks)), dma((2, chunks)), dma((2, chunks)),
+            dma((2, chunks)), dma, dma, dma((3,)), dma((2,)), dma((PLANE - 1,)), dma((PLANE - 1,)),
+            dma((2, chunks)), dma((2, chunks)), dma((2, chunks)), dma((2, chunks)), dma((2, chunks)),
             dma((chunks,)),
         ],
         compiler_params=pltpu.CompilerParams(
             collective_id=0, has_side_effects=True, vmem_limit_bytes=52 * 1024 * 1024
         ),
         name="decayed_attention",
-    )(queries, key_input, value_input, log_decay.T, conv_weight, norm_gain.reshape(1, width))
+    )(*(pltpu.with_memory_space_constraint(x, pltpu.HBM) for x in arguments))
 
 
 def solution(mesh):

time: 33.9 us -> 30.7 us (0.906)
  local copies, waits for them, and re-layouts: 3.25 us -> 0.97 us
  Pallas kernels: 30.3 us -> 29.5 us
    unnamed x7 -> x1, local copies, waits for them, and re-layouts: 3.25 us -> 0.97 us
    pallas_call x1, Pallas kernels: 30.3 us -> 29.5 us  [on_device(): pl.pallas_call(functools.partial(kernel, n), out_shape=jax.ShapeDtypeStru...]
where the time goes in v4:
time: 30.7 us; the launch traced here: 30.5 us
  Pallas kernels  29.5 us (96%)
  local copies, waits for them, and re-layouts  0.97 us (3%)
    pallas_call x1, Pallas kernels, on_device(): pl.pallas_call(functools.partial(kernel, n), out_shape=jax.ShapeDtypeStru...  29.5 us
    unnamed x1, local copies, waits for them, and re-layouts  0.97 us

profile of v4, /device:TPU:27, one launch (start us, length us, event | category | flops | bytes accessed | tf_op | source)
XLA Modules:
  0.0 30.5 jit_solution(564756399629872213)
XLA Ops:
  0.0 29.5 %decayed_attention.1 = bf16[128,4096]{1,0:T(8,128)(2,1)S(1)} custom-call(bf16[128,4096]{1,0:T(8,128)(2,1)} %q_hbm.1, bf16[128,4096]{1,0:T(8,128)(2,1)} %k_hbm.1, bf16[128,4096]{1,0:T(8,128)(2,1)} %v_hbm.1, f32[32,128]{1,0:T(8,128)} %bitcast.2, f32[4,4096]{1,0:T(4,128)} %w_hbm.1, f32[1,4096]{1,0:T(1,128)} %bitcast.3), custom_call_target="tpu_custom_call" | custom-call | tf_op jit(solution)/shard_map/decayed_attention/pallas_call | solution.py:415
  29.5 1.0 %copy.8 = bf16[128,4096]{1,0:T(8,128)(2,1)} copy(bf16[128,4096]{1,0:T(8,128)(2,1)S(1)} %decayed_attention.1) | data formatting | bytes 2097152

commit v5 on v4

--- a/solution.py
+++ b/solution.py
@@ -12,6 +12,7 @@
 BF16 = jnp.bfloat16
 PLANE = 4
 GROUP = 4
+BATCH = 2
 TAIL = 16
 PARTS = 4
 
@@ -46,32 +47,6 @@
     has_before = z > 0
     has_after = z < planes - 1
 
-    def chunk_columns(j):
-        return pl.ds(pl.multiple_of(j * cols, cols), cols)
-
-    def load(source, target, kind, j):
-        here = chunk_columns(j)
-        return pltpu.make_async_copy(source.at[:, here], target.at[:, here], in_sem.at[kind, j])
-
-    small = [
-        pltpu.make_async_copy(source, target, small_sem.at[at])
-        for at, (source, target) in enumerate(((ld_hbm, ld_ref), (w_hbm, w_ref), (g_hbm, g_ref)))
-    ]
-    small[0].start()
-    tail_load = pltpu.make_async_copy(k_hbm.at[pl.ds(rows - TAIL, TAIL), :], tail, tail_sem)
-    tail_load.start()
-    small[1].start()
-
-    def start_loads(j, carry):
-        load(k_hbm, k_s, 0, j).start()
-        load(v_hbm, v_s, 1, j).start()
-        return carry
-
-    lax.fori_loop(0, chunks, start_loads, 0)
-    q_in = pltpu.make_async_copy(q_hbm, q_s, q_sem)
-    q_in.start()
-    small[2].start()
-
     barrier = pltpu.get_barrier_semaphore()
 
     def greet(target):
@@ -90,6 +65,38 @@
         def _(target=target):
             greet(target)
 
+    batches = chunks // BATCH
+    each = [(c, i) for c in range(BATCH) for i in range(GROUP)]
+
+    def chunk_columns(j):
+        return pl.ds(pl.multiple_of(j * cols, cols), cols)
+
+    def batch_columns(b):
+        return pl.ds(pl.multiple_of(b * BATCH * cols, BATCH * cols), BATCH * cols)
+
+    def load(source, target, kind, j):
+        here = batch_columns(j)
+        return pltpu.make_async_copy(source.at[:, here], target.at[:, here], in_sem.at[kind, j])
+
+    small = [
+        pltpu.make_async_copy(source, target, small_sem.at[at])
+        for at, (source, target) in enumerate(((ld_hbm, ld_ref), (w_hbm, w_ref), (g_hbm, g_ref)))
+    ]
+    small[0].start()
+    tail_load = pltpu.make_async_copy(k_hbm.at[pl.ds(rows - TAIL, TAIL), :], tail, tail_sem)
+    tail_load.start()
+    small[1].start()
+
+    def start_loads(j, carry):
+        load(k_hbm, k_s, 0, j).start()
+        load(v_hbm, v_s, 1, j).start()
+        return carry
+
+    lax.fori_loop(0, batches, start_loads, 0)
+    q_in = pltpu.make_async_copy(q_hbm, q_s, q_sem)
+    q_in.start()
+    small[2].start()
+
     t_at = lax.broadcasted_iota(jnp.int32, (rows, rows), 0)
     s_at = lax.broadcasted_iota(jnp.int32, (rows, rows), 1)
     lower = jnp.where(s_at <= t_at, 1.0, 0.0).astype(F32)
@@ -218,28 +225,28 @@
     def head_columns(j, i):
         return pl.ds(pl.multiple_of(j * cols + i * size, size), size)
 
-    def states(j):
-        load(k_hbm, k_s, 0, j).wait()
-        load(v_hbm, v_s, 1, j).wait()
-        wide = chunk_columns(j)
+    def states(b):
+        load(k_hbm, k_s, 0, b).wait()
+        load(v_hbm, v_s, 1, b).wait()
+        wide = batch_columns(b)
         kx[0:8, :] = halo[:, wide]
         kx[pl.ds(8, rows), :] = k_s[:, wide].astype(F32)
-        taps_j = w_ref[:, wide]
-        fade = [fade_t[pl.ds(j * GROUP + i, 1), :] for i in range(GROUP)]
-        values = [v_s[:, head_columns(j, i)] for i in range(GROUP)]
+        taps_b = w_ref[:, wide]
+        fade = [fade_t[pl.ds((b * BATCH + c) * GROUP + i, 1), :] for c, i in each]
+        values = [v_s[:, head_columns(b * BATCH + c, i)] for c, i in each]
         turned = []
-        for i in range(GROUP):
-            near = slice(i * size, (i + 1) * size)
-            total = taps_j[0:1, near] * kx[pl.ds(8, rows), near]
+        for c, i in each:
+            near = slice((c * GROUP + i) * size, (c * GROUP + i + 1) * size)
+            total = taps_b[0:1, near] * kx[pl.ds(8, rows), near]
             for tap in range(1, taps):
-                total = total + taps_j[tap : tap + 1, near] * kx[pl.ds(8 - tap, rows), near]
-            turned.append(total.T.astype(BF16))
-        weighted = [(turned[i].astype(F32) * fade[i]).astype(BF16) for i in range(GROUP)]
-        state = [dot(weighted[i], values[i], ((1,), (0,))) for i in range(GROUP)]
-        for i in range(GROUP):
-            kc_s[j, i] = turned[i]
-            s_all[j, i] = state[i]
-            s_low[j, i] = state[i].astype(BF16)
+                total = total + taps_b[tap : tap + 1, near] * kx[pl.ds(8 - tap, rows), near]
+            turned.append(total.astype(BF16).T)
+        weighted = [(t.astype(F32) * f).astype(BF16) for t, f in zip(turned, fade)]
+        state = [dot(w, v, ((1,), (0,))) for w, v in zip(weighted, values)]
+        for at, (c, i) in enumerate(each):
+            kc_s[b * BATCH + c, i] = turned[at]
+            s_all[b * BATCH + c, i] = state[at]
+            s_low[b * BATCH + c, i] = state[at].astype(BF16)
 
     def ordered(flag, mine, other):
         return jnp.where(flag, mine, other), jnp.where(flag, other, mine)
@@ -252,19 +259,21 @@
             s_chip[j, a] = joined
         y_send[j] = s_chip[j, 1 - y].astype(BF16)
 
-    def within(j):
-        cum_j = cum_c[j][:, 0:GROUP]
-        each = range(GROUP)
-        scores = [dot(q_s[:, head_columns(j, i)], kc_s[j, i], ((1,), (0,))) for i in each]
-        values = [v_s[:, head_columns(j, i)] for i in each]
-        ahead = [cum_t[pl.ds(j * GROUP + i, 1), :] for i in each]
+    def within(b):
+        cum_b = [cum_c[b * BATCH + c][:, 0:GROUP] for c in range(BATCH)]
+        queries = [q_s[:, head_columns(b * BATCH + c, i)] for c, i in each]
+        values = [v_s[:, head_columns(b * BATCH + c, i)] for c, i in each]
+        ahead = [cum_t[pl.ds((b * BATCH + c) * GROUP + i, 1), :] for c, i in each]
+        scores = [
+            dot(queries[at], kc_s[b * BATCH + c, i], ((1,), (0,))) for at, (c, i) in enumerate(each)
+        ]
         weights = []
-        for i in each:
-            spread = jnp.where(s_at <= t_at, cum_j[:, i : i + 1] - ahead[i], -1e30)
-            weights.append((scores[i] * jnp.exp(spread)).astype(BF16))
-        intra = [dot(weights[i], values[i], ((1,), (0,))) for i in each]
-        for i in each:
-            intra_s[:, head_columns(j, i)] = intra[i]
+        for at, (c, i) in enumerate(each):
+            spread = jnp.where(s_at <= t_at, cum_b[c][:, i : i + 1] - ahead[at], -1e30)
+            weights.append((scores[at] * jnp.exp(spread)).astype(BF16))
+        intra = [dot(w, v, ((1,), (0,))) for w, v in zip(weights, values)]
+        for at, (c, i) in enumerate(each):
+            intra_s[:, head_columns(b * BATCH + c, i)] = intra[at]
 
     def advance(j):
         h = pl.ds(j * GROUP + 2 * core + y, 1)
@@ -286,37 +295,49 @@
             pre[j, 2 * core + a] = mine.astype(BF16)
             b_send[j, a] = other.astype(BF16)
 
-    def finish(j):
-        grow = jnp.exp(cum_c[j][:, 0:GROUP])
-        gain = g_ref[:, chunk_columns(j)]
-        each = range(GROUP)
-        inter = [dot(q_s[:, head_columns(j, i)], pre[j, i], ((1,), (0,))) for i in each]
-        intra = [intra_s[:, head_columns(j, i)] for i in each]
-        mixed = [intra[i] + inter[i] * grow[:, i : i + 1] for i in each]
-        scale = [
-            lax.rsqrt(jnp.mean(mixed[i] * mixed[i], axis=1, keepdims=True) + 1e-05) for i in each
+    def finish(b):
+        grow = [jnp.exp(cum_c[b * BATCH + c][:, 0:GROUP]) for c in range(BATCH)]
+        gain = g_ref[:, batch_columns(b)]
+        queries = [q_s[:, head_columns(b * BATCH + c, i)] for c, i in each]
+        intra = [intra_s[:, head_columns(b * BATCH + c, i)] for c, i in each]
+        inter = [
+            dot(queries[at], pre[b * BATCH + c, i], ((1,), (0,))) for at, (c, i) in enumerate(each)
         ]
+        mixed = [
+            intra[at] + inter[at] * grow[c][:, i : i + 1] for at, (c, i) in enumerate(each)
+        ]
+        scale = [lax.rsqrt(jnp.mean(m * m, axis=1, keepdims=True) + 1e-05) for m in mixed]
         result = [
-            (mixed[i] * scale[i] * gain[:, i * size : (i + 1) * size]).astype(BF16) for i in each
+            (mixed[at] * scale[at] * gain[:, at * size : (at + 1) * size]).astype(BF16)
+            for at in range(len(each))
         ]
-        for i in each:
-            out_s[:, head_columns(j, i)] = result[i]
-
-    chain_lag = jnp.minimum(4 + lax.div(5 * z, 2), chunks + 3)
-    within_lag = jnp.where(z < 2, chunks, chunks // 2)
-    prefix_lag = chain_lag + 3
-    finish_lag = jnp.maximum(prefix_lag + 2, within_lag + 1)
+        for at, (c, i) in enumerate(each):
+            out_s[:, head_columns(b * BATCH + c, i)] = result[at]
+
+    chain_lag = jnp.minimum(2 + 2 * z, 2 * batches)
+    within_lag = jnp.where(z == 0, batches + 2, jnp.where(z == 1, batches + 3, batches))
+    prefix_lag = jnp.maximum(
+        chain_lag + 1, jnp.where(z == 0, batches + 2, jnp.where(z == 1, 2 * batches, 0))
+    )
+    finish_lag = jnp.maximum(prefix_lag, within_lag) + 1
 
     def during(step, lag, work):
-        j = step - lag
-
-        @pl.when(jnp.logical_and(j >= 0, j < chunks))
-        def _():
-            work(j)
-
-    def state_part(j):
-        states(j)
-        x_copy(j).start()
+        b = step - lag
+
+        @pl.when(jnp.logical_and(b >= 0, b < batches))
+        def _():
+            work(b)
+
+    def per_chunk(work):
+        def run(b):
+            for c in range(BATCH):
+                work(b * BATCH + c)
+
+        return run
+
+    def state_part(b):
+        states(b)
+        per_chunk(lambda j: x_copy(j).start())(b)
 
     def chip_part(j):
         x_copy(j).wait_recv()
@@ -343,18 +364,18 @@
         prefixes(j)
         b_copy(j, core).start()
 
-    def within_part(j):
-        @pl.when(j == 0)
+    def within_part(b):
+        @pl.when(b == 0)
         def _():
             q_in.wait()
             small[2].wait()
 
-        within(j)
-
-    def finish_part(j):
-        b_copy(j, 1 - core).wait_recv()
-        finish(j)
-        out_copy(j).start()
+        within(b)
+
+    def finish_part(b):
+        per_chunk(lambda j: b_copy(j, 1 - core).wait_recv())(b)
+        finish(b)
+        per_chunk(lambda j: out_copy(j).start())(b)
 
     def one_step(step, carry):
         during(step, 0, state_part)
@@ -367,14 +388,14 @@
             coef[1] = dec[2] * dec[3]
             coef[2] = dec[0] * dec[1] * (dec[2] * dec[3])
 
-        during(step, 1, chip_part)
-        during(step, chain_lag, chain_part)
-        during(step, prefix_lag, prefix_part)
+        during(step, 1, per_chunk(chip_part))
+        during(step, chain_lag, per_chunk(chain_part))
+        during(step, prefix_lag, per_chunk(prefix_part))
         during(step, within_lag, within_part)
         during(step, finish_lag, finish_part)
         return carry
 
-    lax.fori_loop(0, 2 * chunks + 8, one_step, 0)
+    lax.fori_loop(0, 3 * batches + 3, one_step, 0)
 
     def drain(j, carry):
         x_copy(j).wait_send()
@@ -426,7 +447,7 @@
             pltpu.VMEM((TAIL, width // PARTS), BF16),
             pltpu.VMEM((TAIL, width // PARTS), BF16),
             pltpu.VMEM((8, width), F32),
-            pltpu.VMEM((rows + 8, GROUP * size), F32),
+            pltpu.VMEM((rows + 8, BATCH * GROUP * size), F32),
             pltpu.VMEM((chunks, GROUP, size, rows), BF16),
             pltpu.VMEM((rows, width), F32),
             pltpu.VMEM((chunks, rows, size), F32),
@@ -438,7 +459,7 @@
             pltpu.VMEM((chunks, GROUP, size, size), BF16),
             pair, pair_wide, one, one, one, one, one, pair, pair,
             pltpu.VMEM((chunks, GROUP, size, size), BF16),
-            dma((2, chunks)), dma, dma, dma((3,)), dma((2,)), dma((PLANE - 1,)), dma((PLANE - 1,)),
+            dma((2, chunks // BATCH)), dma, dma, dma((3,)), dma((2,)), dma((PLANE - 1,)), dma((PLANE - 1,)),
             dma((2, chunks)), dma((2, chunks)), dma((2, chunks)), dma((2, chunks)), dma((2, chunks)),
             dma((chunks,)),
         ],

time: 30.7 us -> 30.7 us (level)
  no operation moved by 1% of the time
where the time goes in v5:
time: 30.7 us; the launch traced here: 30.5 us
  Pallas kernels  29.5 us (96%)
  local copies, waits for them, and re-layouts  0.97 us (3%)
    pallas_call x1, Pallas kernels, on_device(): pl.pallas_call(functools.partial(kernel, n), out_shape=jax.ShapeDtypeStru...  29.5 us
    unnamed x1, local copies, waits for them, and re-layouts  0.97 us

profile of v5, /device:TPU:27, one launch (start us, length us, event | category | flops | bytes accessed | tf_op | source)
XLA Modules:
  0.0 30.5 jit_solution(11764769024121855197)
XLA Ops:
  0.0 29.5 %decayed_attention.1 = bf16[128,4096]{1,0:T(8,128)(2,1)S(1)} custom-call(bf16[128,4096]{1,0:T(8,128)(2,1)} %q_hbm.1, bf16[128,4096]{1,0:T(8,128)(2,1)} %k_hbm.1, bf16[128,4096]{1,0:T(8,128)(2,1)} %v_hbm.1, f32[32,128]{1,0:T(8,128)} %bitcast.2, f32[4,4096]{1,0:T(4,128)} %w_hbm.1, f32[1,4096]{1,0:T(1,128)} %bitcast.3), custom_call_target="tpu_custom_call" | custom-call | tf_op jit(solution)/shard_map/decayed_attention/pallas_call | solution.py:436
  29.5 1.0 %copy.8 = bf16[128,4096]{1,0:T(8,128)(2,1)} copy(bf16[128,4096]{1,0:T(8,128)(2,1)S(1)} %decayed_attention.1) | data formatting | bytes 2097152

commit v6 on v5

--- a/solution.py
+++ b/solution.py
@@ -97,6 +97,33 @@
     q_in.start()
     small[2].start()
 
+    keep = taps - 1
+    part = width // PARTS
+    tail_load.wait()
+    last = tail[...].astype(F32)[TAIL - keep : TAIL]
+    packed = [last[:, p * part : (p + 1) * part] for p in range(PARTS)]
+    packed.append(jnp.zeros((TAIL - PARTS * keep, part), F32))
+    tail_out[...] = jnp.concatenate(packed, axis=0).astype(BF16)
+
+    guests = PLANE - 1
+    for there, _ in links:
+        guests = guests + jnp.where(there, 1, 0)
+    pl.semaphore_wait(barrier, guests)
+
+    def halo_copy(target):
+        return pltpu.make_async_remote_copy(
+            src_ref=tail_out,
+            dst_ref=tail_in,
+            send_sem=halo_sem.at[0],
+            recv_sem=halo_sem.at[1],
+            device_id={"ctx": target},
+            device_id_type=MESH,
+        )
+
+    @pl.when(me < n - 1)
+    def _():
+        halo_copy(me + 1).start()
+
     t_at = lax.broadcasted_iota(jnp.int32, (rows, rows), 0)
     s_at = lax.broadcasted_iota(jnp.int32, (rows, rows), 1)
     lower = jnp.where(s_at <= t_at, 1.0, 0.0).astype(F32)
@@ -111,32 +138,6 @@
     dec[r] = jnp.broadcast_to(jnp.exp(cum_rows[:, rows - 1 : rows]), (heads, size))
 
     fade_t[...] = jnp.exp(cum_rows[:, rows - 1 : rows] - cum_rows)
-    keep = taps - 1
-    part = width // PARTS
-    tail_load.wait()
-    last = tail[...].astype(F32)[TAIL - keep : TAIL]
-    packed = [last[:, p * part : (p + 1) * part] for p in range(PARTS)]
-    packed.append(jnp.zeros((TAIL - PARTS * keep, part), F32))
-    tail_out[...] = jnp.concatenate(packed, axis=0).astype(BF16)
-
-    guests = PLANE - 1
-    for there, _ in links:
-        guests = guests + jnp.where(there, 1, 0)
-    pl.semaphore_wait(barrier, guests)
-
-    def halo_copy(target):
-        return pltpu.make_async_remote_copy(
-            src_ref=tail_out,
-            dst_ref=tail_in,
-            send_sem=halo_sem.at[0],
-            recv_sem=halo_sem.at[1],
-            device_id={"ctx": target},
-            device_id_type=MESH,
-        )
-
-    @pl.when(me < n - 1)
-    def _():
-        halo_copy(me + 1).start()
 
     def dec_copy(off, slot):
         return pltpu.make_async_remote_copy(
@@ -314,11 +315,9 @@
         for at, (c, i) in enumerate(each):
             out_s[:, head_columns(b * BATCH + c, i)] = result[at]
 
-    chain_lag = jnp.minimum(2 + 2 * z, 2 * batches)
-    within_lag = jnp.where(z == 0, batches + 2, jnp.where(z == 1, batches + 3, batches))
-    prefix_lag = jnp.maximum(
-        chain_lag + 1, jnp.where(z == 0, batches + 2, jnp.where(z == 1, 2 * batches, 0))
-    )
+    chain_lag = jnp.where(z == 0, 3, jnp.minimum(2 + 2 * z, 2 * batches))
+    within_lag = jnp.where(z == 0, batches + 2, jnp.where(z == 1, batches + 3, batches - 1))
+    prefix_lag = jnp.where(z < 2, batches + 3 + z, chain_lag + 2)
     finish_lag = jnp.maximum(prefix_lag, within_lag) + 1
 
     def during(step, lag, work):
@@ -380,7 +379,7 @@
     def one_step(step, carry):
         during(step, 0, state_part)
 
-        @pl.when(step == 0)
+        @pl.when(step == 1)
         def _():
             for off in range(1, PLANE):
                 dec_copy(off, lax.rem(r - off + PLANE, PLANE)).wait_recv()
@@ -395,7 +394,7 @@
         during(step, finish_lag, finish_part)
         return carry
 
-    lax.fori_loop(0, 3 * batches + 3, one_step, 0)
+    lax.fori_loop(0, 3 * batches + 5, one_step, 0)
 
     def drain(j, carry):
         x_copy(j).wait_send()

time: 30.7 us -> 29.1 us (0.948)
  Pallas kernels: 29.5 us -> 28 us
    pallas_call x1, Pallas kernels: 29.5 us -> 28 us  [on_device(): pl.pallas_call(functools.partial(kernel, n), out_shape=jax.ShapeDtypeStru...]
where the time goes in v6:
time: 29.1 us; the launch traced here: 29 us
  Pallas kernels  28 us (96%)
  local copies, waits for them, and re-layouts  0.97 us (3%)
    pallas_call x1, Pallas kernels, on_device(): pl.pallas_call(functools.partial(kernel, n), out_shape=jax.ShapeDtypeStru...  28 us
    unnamed x1, local copies, waits for them, and re-layouts  0.97 us

profile of v6, /device:TPU:27, one launch (start us, length us, event | category | flops | bytes accessed | tf_op | source)
XLA Modules:
  0.0 29.0 jit_solution(5386552400032328134)
XLA Ops:
  0.0 28.0 %decayed_attention.1 = bf16[128,4096]{1,0:T(8,128)(2,1)S(1)} custom-call(bf16[128,4096]{1,0:T(8,128)(2,1)} %q_hbm.1, bf16[128,4096]{1,0:T(8,128)(2,1)} %k_hbm.1, bf16[128,4096]{1,0:T(8,128)(2,1)} %v_hbm.1, f32[32,128]{1,0:T(8,128)} %bitcast.2, f32[4,4096]{1,0:T(4,128)} %w_hbm.1, f32[1,4096]{1,0:T(1,128)} %bitcast.3), custom_call_target="tpu_custom_call" | custom-call | tf_op jit(solution)/shard_map/decayed_attention/pallas_call | solution.py:435
  28.0 1.0 %copy.8 = bf16[128,4096]{1,0:T(8,128)(2,1)} copy(bf16[128,4096]{1,0:T(8,128)(2,1)S(1)} %decayed_attention.1) | data formatting | bytes 2097152

commit v7 on v6

--- a/solution.py
+++ b/solution.py
@@ -226,6 +226,10 @@
     def head_columns(j, i):
         return pl.ds(pl.multiple_of(j * cols + i * size, size), size)
 
+    f_at = lax.broadcasted_iota(jnp.int32, (size, size), 0)
+    g_at = lax.broadcasted_iota(jnp.int32, (size, size), 1)
+    unit = jnp.where(f_at == g_at, 1.0, 0.0).astype(BF16)
+
     def states(b):
         load(k_hbm, k_s, 0, b).wait()
         load(v_hbm, v_s, 1, b).wait()
@@ -235,17 +239,18 @@
         taps_b = w_ref[:, wide]
         fade = [fade_t[pl.ds((b * BATCH + c) * GROUP + i, 1), :] for c, i in each]
         values = [v_s[:, head_columns(b * BATCH + c, i)] for c, i in each]
-        turned = []
+        conv = []
         for c, i in each:
             near = slice((c * GROUP + i) * size, (c * GROUP + i + 1) * size)
             total = taps_b[0:1, near] * kx[pl.ds(8, rows), near]
             for tap in range(1, taps):
                 total = total + taps_b[tap : tap + 1, near] * kx[pl.ds(8 - tap, rows), near]
-            turned.append(total.astype(BF16).T)
-        weighted = [(t.astype(F32) * f).astype(BF16) for t, f in zip(turned, fade)]
+            conv.append(total.astype(BF16))
+        turned = [dot(unit, c, ((1,), (1,))) for c in conv]
+        weighted = [(t * f).astype(BF16) for t, f in zip(turned, fade)]
         state = [dot(w, v, ((1,), (0,))) for w, v in zip(weighted, values)]
         for at, (c, i) in enumerate(each):
-            kc_s[b * BATCH + c, i] = turned[at]
+            kc_s[b * BATCH + c, i] = conv[at]
             s_all[b * BATCH + c, i] = state[at]
             s_low[b * BATCH + c, i] = state[at].astype(BF16)
 
@@ -266,7 +271,7 @@
         values = [v_s[:, head_columns(b * BATCH + c, i)] for c, i in each]
         ahead = [cum_t[pl.ds((b * BATCH + c) * GROUP + i, 1), :] for c, i in each]
         scores = [
-            dot(queries[at], kc_s[b * BATCH + c, i], ((1,), (0,))) for at, (c, i) in enumerate(each)
+            dot(queries[at], kc_s[b * BATCH + c, i], ((1,), (1,))) for at, (c, i) in enumerate(each)
         ]
         weights = []
         for at, (c, i) in enumerate(each):
@@ -447,7 +452,7 @@
             pltpu.VMEM((TAIL, width // PARTS), BF16),
             pltpu.VMEM((8, width), F32),
             pltpu.VMEM((rows + 8, BATCH * GROUP * size), F32),
-            pltpu.VMEM((chunks, GROUP, size, rows), BF16),
+            pltpu.VMEM((chunks, GROUP, rows, size), BF16),
             pltpu.VMEM((rows, width), F32),
             pltpu.VMEM((chunks, rows, size), F32),
             pltpu.VMEM((heads, rows), F32),

time: 29.1 us -> 29.1 us (level)
  no operation moved by 1% of the time
where the time goes in v7:
time: 29.1 us; the launch traced here: 28.9 us
  Pallas kernels  28 us (96%)
  local copies, waits for them, and re-layouts  0.97 us (3%)
    pallas_call x1, Pallas kernels, on_device(): pl.pallas_call(functools.partial(kernel, n), out_shape=jax.ShapeDtypeStru...  28 us
    unnamed x1, local copies, waits for them, and re-layouts  0.97 us

profile of v7, /device:TPU:27, one launch (start us, length us, event | category | flops | bytes accessed | tf_op | source)
XLA Modules:
  0.0 28.9 jit_solution(9198158787684365905)
XLA Ops:
  0.0 28.0 %decayed_attention.1 = bf16[128,4096]{1,0:T(8,128)(2,1)S(1)} custom-call(bf16[128,4096]{1,0:T(8,128)(2,1)} %q_hbm.1, bf16[128,4096]{1,0:T(8,128)(2,1)} %k_hbm.1, bf16[128,4096]{1,0:T(8,128)(2,1)} %v_hbm.1, f32[32,128]{1,0:T(8,128)} %bitcast.2, f32[4,4096]{1,0:T(4,128)} %w_hbm.1, f32[1,4096]{1,0:T(1,128)} %bitcast.3), custom_call_target="tpu_custom_call" | custom-call | tf_op jit(solution)/shard_map/decayed_attention/pallas_call | solution.py:440
  28.0 1.0 %copy.8 = bf16[128,4096]{1,0:T(8,128)(2,1)} copy(bf16[128,4096]{1,0:T(8,128)(2,1)S(1)} %decayed_attention.1) | data formatting | bytes 2097152

commit v8 on v7

--- a/solution.py
+++ b/solution.py
@@ -278,8 +278,14 @@
             spread = jnp.where(s_at <= t_at, cum_b[c][:, i : i + 1] - ahead[at], -1e30)
             weights.append((scores[at] * jnp.exp(spread)).astype(BF16))
         intra = [dot(w, v, ((1,), (0,))) for w, v in zip(weights, values)]
+        grow = [jnp.exp(c) for c in cum_b]
+        grown = [
+            (queries[at].astype(F32) * grow[c][:, i : i + 1]).astype(BF16)
+            for at, (c, i) in enumerate(each)
+        ]
         for at, (c, i) in enumerate(each):
             intra_s[:, head_columns(b * BATCH + c, i)] = intra[at]
+            q_s[:, head_columns(b * BATCH + c, i)] = grown[at]
 
     def advance(j):
         h = pl.ds(j * GROUP + 2 * core + y, 1)
@@ -287,6 +293,11 @@
         before = z_recv[j].astype(F32)
         plane = coef[1, h, :] * first + second
         z_send[j] = (coef[2, h, :] * before + plane).astype(BF16)
+
+        @pl.when(has_after)
+        def _():
+            z_copy(j).start()
+
         mine, other = ordered(y == 0, before, coef[0, h, :] * before + first)
         r_send[j] = other.astype(BF16)
         base[j, y] = mine.astype(BF16)
@@ -302,16 +313,13 @@
             b_send[j, a] = other.astype(BF16)
 
     def finish(b):
-        grow = [jnp.exp(cum_c[b * BATCH + c][:, 0:GROUP]) for c in range(BATCH)]
         gain = g_ref[:, batch_columns(b)]
         queries = [q_s[:, head_columns(b * BATCH + c, i)] for c, i in each]
         intra = [intra_s[:, head_columns(b * BATCH + c, i)] for c, i in each]
         inter = [
             dot(queries[at], pre[b * BATCH + c, i], ((1,), (0,))) for at, (c, i) in enumerate(each)
         ]
-        mixed = [
-            intra[at] + inter[at] * grow[c][:, i : i + 1] for at, (c, i) in enumerate(each)
-        ]
+        mixed = [x + y for x, y in zip(intra, inter)]
         scale = [lax.rsqrt(jnp.mean(m * m, axis=1, keepdims=True) + 1e-05) for m in mixed]
         result = [
             (mixed[at] * scale[at] * gain[:, at * size : (at + 1) * size]).astype(BF16)
@@ -356,11 +364,6 @@
             z_copy(j).wait_recv()
 
         advance(j)
-
-        @pl.when(has_after)
-        def _():
-            z_copy(j).start()
-
         r_copy(j, y).start()
 
     def prefix_part(j):

time: 29.1 us -> 29 us (level)
  no operation moved by 1% of the time
where the time goes in v8:
time: 29 us; the launch traced here: 28.9 us
  Pallas kernels  27.9 us (96%)
  local copies, waits for them, and re-layouts  0.97 us (3%)
    pallas_call x1, Pallas kernels, on_device(): pl.pallas_call(functools.partial(kernel, n), out_shape=jax.ShapeDtypeStru...  27.9 us
    unnamed x1, local copies, waits for them, and re-layouts  0.97 us

profile of v8, /device:TPU:27, one launch (start us, length us, event | category | flops | bytes accessed | tf_op | source)
XLA Modules:
  0.0 28.9 jit_solution(1633223904311308355)
XLA Ops:
  0.0 27.9 %decayed_attention.1 = bf16[128,4096]{1,0:T(8,128)(2,1)S(1)} custom-call(bf16[128,4096]{1,0:T(8,128)(2,1)} %q_hbm.1, bf16[128,4096]{1,0:T(8,128)(2,1)} %k_hbm.1, bf16[128,4096]{1,0:T(8,128)(2,1)} %v_hbm.1, f32[32,128]{1,0:T(8,128)} %bitcast.2, f32[4,4096]{1,0:T(4,128)} %w_hbm.1, f32[1,4096]{1,0:T(1,128)} %bitcast.3), custom_call_target="tpu_custom_call" | custom-call | tf_op jit(solution)/shard_map/decayed_attention/pallas_call | solution.py:443
  27.9 1.0 %copy.8 = bf16[128,4096]{1,0:T(8,128)(2,1)} copy(bf16[128,4096]{1,0:T(8,128)(2,1)S(1)} %decayed_attention.1) | data formatting | bytes 2097152

commit v9 on v8

--- a/solution.py
+++ b/solution.py
@@ -152,10 +152,13 @@
     for off in range(1, PLANE):
         dec_copy(off, r).start()
 
+    def span(b):
+        return pl.ds(b * BATCH, BATCH)
+
     def x_copy(j):
         return pltpu.make_async_remote_copy(
-            src_ref=s_low.at[j, pl.ds(2 * (1 - core), 2)],
-            dst_ref=x_recv.at[j],
+            src_ref=s_low.at[span(j), pl.ds(2 * (1 - core), 2)],
+            dst_ref=x_recv.at[span(j)],
             send_sem=x_sem.at[0, j],
             recv_sem=x_sem.at[1, j],
             device_id={"ctx": sibling},
@@ -164,8 +167,8 @@
 
     def y_copy(j):
         return pltpu.make_async_remote_copy(
-            src_ref=y_send.at[j],
-            dst_ref=y_recv.at[j],
+            src_ref=y_send.at[span(j)],
+            dst_ref=y_recv.at[span(j)],
             send_sem=y_sem.at[0, j],
             recv_sem=y_sem.at[1, j],
             device_id={"ctx": across},
@@ -174,8 +177,8 @@
 
     def z_copy(j):
         return pltpu.make_async_remote_copy(
-            src_ref=z_send.at[j],
-            dst_ref=z_recv.at[j],
+            src_ref=z_send.at[span(j)],
+            dst_ref=z_recv.at[span(j)],
             send_sem=z_sem.at[0, j],
             recv_sem=z_sem.at[1, j],
             device_id={"ctx": me + PLANE},
@@ -184,8 +187,8 @@
 
     def r_copy(j, owner):
         return pltpu.make_async_remote_copy(
-            src_ref=r_send.at[j],
-            dst_ref=base.at[j, owner],
+            src_ref=r_send.at[span(j)],
+            dst_ref=base.at[span(j), owner],
             send_sem=r_sem.at[0, j],
             recv_sem=r_sem.at[1, j],
             device_id={"ctx": across},
@@ -194,8 +197,8 @@
 
     def b_copy(j, owner):
         return pltpu.make_async_remote_copy(
-            src_ref=b_send.at[j],
-            dst_ref=pre.at[j, pl.ds(2 * owner, 2)],
+            src_ref=b_send.at[span(j)],
+            dst_ref=pre.at[span(j), pl.ds(2 * owner, 2)],
             send_sem=b_sem.at[0, j],
             recv_sem=b_sem.at[1, j],
             device_id={"ctx": sibling},
@@ -293,11 +296,6 @@
         before = z_recv[j].astype(F32)
         plane = coef[1, h, :] * first + second
         z_send[j] = (coef[2, h, :] * before + plane).astype(BF16)
-
-        @pl.when(has_after)
-        def _():
-            z_copy(j).start()
-
         mine, other = ordered(y == 0, before, coef[0, h, :] * before + first)
         r_send[j] = other.astype(BF16)
         base[j, y] = mine.astype(BF16)
@@ -349,27 +347,32 @@
 
     def state_part(b):
         states(b)
-        per_chunk(lambda j: x_copy(j).start())(b)
-
-    def chip_part(j):
-        x_copy(j).wait_recv()
-        chip_states(j)
-        y_copy(j).start()
-
-    def chain_part(j):
-        y_copy(j).wait_recv()
+        x_copy(b).start()
+
+    def chip_part(b):
+        x_copy(b).wait_recv()
+        per_chunk(chip_states)(b)
+        y_copy(b).start()
+
+    def chain_part(b):
+        y_copy(b).wait_recv()
 
         @pl.when(has_before)
         def _():
-            z_copy(j).wait_recv()
-
-        advance(j)
-        r_copy(j, y).start()
-
-    def prefix_part(j):
-        r_copy(j, 1 - y).wait_recv()
-        prefixes(j)
-        b_copy(j, core).start()
+            z_copy(b).wait_recv()
+
+        per_chunk(advance)(b)
+
+        @pl.when(has_after)
+        def _():
+            z_copy(b).start()
+
+        r_copy(b, y).start()
+
+    def prefix_part(b):
+        r_copy(b, 1 - y).wait_recv()
+        per_chunk(prefixes)(b)
+        b_copy(b, core).start()
 
     def within_part(b):
         @pl.when(b == 0)
@@ -380,7 +383,7 @@
         within(b)
 
     def finish_part(b):
-        per_chunk(lambda j: b_copy(j, 1 - core).wait_recv())(b)
+        b_copy(b, 1 - core).wait_recv()
         finish(b)
         per_chunk(lambda j: out_copy(j).start())(b)
 
@@ -395,9 +398,9 @@
             coef[1] = dec[2] * dec[3]
             coef[2] = dec[0] * dec[1] * (dec[2] * dec[3])
 
-        during(step, 1, per_chunk(chip_part))
-        during(step, chain_lag, per_chunk(chain_part))
-        during(step, prefix_lag, per_chunk(prefix_part))
+        during(step, 1, chip_part)
+        during(step, chain_lag, chain_part)
+        during(step, prefix_lag, prefix_part)
         during(step, within_lag, within_part)
         during(step, finish_lag, finish_part)
         return carry
@@ -414,10 +417,10 @@
         def _():
             z_copy(j).wait_send()
 
-        out_copy(j).wait()
+        per_chunk(lambda c: out_copy(c).wait())(j)
         return carry
 
-    lax.fori_loop(0, chunks, drain, 0)
+    lax.fori_loop(0, batches, drain, 0)
     for off in range(1, PLANE):
         dec_copy(off, r).wait_send()
 

time: 29 us -> 30.4 us (1.048)
  Pallas kernels: 27.9 us -> 29.2 us
    pallas_call x1, Pallas kernels: 27.9 us -> 29.2 us  [on_device(): pl.pallas_call(functools.partial(kernel, n), out_shape=jax.ShapeDtypeStru...]
where the time goes in v9:
time: 30.4 us; the launch traced here: 30.2 us
  Pallas kernels  29.2 us (96%)
  local copies, waits for them, and re-layouts  0.97 us (3%)
    pallas_call x1, Pallas kernels, on_device(): pl.pallas_call(functools.partial(kernel, n), out_shape=jax.ShapeDtypeStru...  29.2 us
    unnamed x1, local copies, waits for them, and re-layouts  0.97 us

profile of v9, /device:TPU:27, one launch (start us, length us, event | category | flops | bytes accessed | tf_op | source)
XLA Modules:
  0.0 30.2 jit_solution(12881538088138390149)
XLA Ops:
  0.0 29.2 %decayed_attention.1 = bf16[128,4096]{1,0:T(8,128)(2,1)S(1)} custom-call(bf16[128,4096]{1,0:T(8,128)(2,1)} %q_hbm.1, bf16[128,4096]{1,0:T(8,128)(2,1)} %k_hbm.1, bf16[128,4096]{1,0:T(8,128)(2,1)} %v_hbm.1, f32[32,128]{1,0:T(8,128)} %bitcast.2, f32[4,4096]{1,0:T(4,128)} %w_hbm.1, f32[1,4096]{1,0:T(1,128)} %bitcast.3), custom_call_target="tpu_custom_call" | custom-call | tf_op jit(solution)/shard_map/decayed_attention/pallas_call | solution.py:446
  29.2 1.0 %copy.8 = bf16[128,4096]{1,0:T(8,128)(2,1)} copy(bf16[128,4096]{1,0:T(8,128)(2,1)S(1)} %decayed_attention.1) | data formatting | bytes 2097152

commit v10 on v8

--- a/solution.py
+++ b/solution.py
@@ -330,7 +330,7 @@
 
     chain_lag = jnp.where(z == 0, 3, jnp.minimum(2 + 2 * z, 2 * batches))
     within_lag = jnp.where(z == 0, batches + 2, jnp.where(z == 1, batches + 3, batches - 1))
-    prefix_lag = jnp.where(z < 2, batches + 3 + z, chain_lag + 2)
+    prefix_lag = jnp.where(z < 2, batches + 3 + z, chain_lag + jnp.where(has_after, 2, 1))
     finish_lag = jnp.maximum(prefix_lag, within_lag) + 1
 
     def during(step, lag, work):

time: 29 us -> 29.5 us (1.017)
  Pallas kernels: 27.9 us -> 28.4 us
    pallas_call x1, Pallas kernels: 27.9 us -> 28.4 us  [on_device(): pl.pallas_call(functools.partial(kernel, n), out_shape=jax.ShapeDtypeStru...]
where the time goes in v10:
time: 29.5 us; the launch traced here: 29.3 us
  Pallas kernels  28.4 us (96%)
  local copies, waits for them, and re-layouts  0.97 us (3%)
    pallas_call x1, Pallas kernels, on_device(): pl.pallas_call(functools.partial(kernel, n), out_shape=jax.ShapeDtypeStru...  28.4 us
    unnamed x1, local copies, waits for them, and re-layouts  0.97 us

profile of v10, /device:TPU:27, one launch (start us, length us, event | category | flops | bytes accessed | tf_op | source)
XLA Modules:
  0.0 29.3 jit_solution(6524838146610434948)
XLA Ops:
  0.0 28.4 %decayed_attention.1 = bf16[128,4096]{1,0:T(8,128)(2,1)S(1)} custom-call(bf16[128,4096]{1,0:T(8,128)(2,1)} %q_hbm.1, bf16[128,4096]{1,0:T(8,128)(2,1)} %k_hbm.1, bf16[128,4096]{1,0:T(8,128)(2,1)} %v_hbm.1, f32[32,128]{1,0:T(8,128)} %bitcast.2, f32[4,4096]{1,0:T(4,128)} %w_hbm.1, f32[1,4096]{1,0:T(1,128)} %bitcast.3), custom_call_target="tpu_custom_call" | custom-call | tf_op jit(solution)/shard_map/decayed_attention/pallas_call | solution.py:443
  28.4 1.0 %copy.8 = bf16[128,4096]{1,0:T(8,128)(2,1)} copy(bf16[128,4096]{1,0:T(8,128)(2,1)S(1)} %decayed_attention.1) | data formatting | bytes 2097152
